TPU v7x, 256 devices: a whole 4x4x8 slice. The times are simulated.
256 devices in a mesh: row: 64 (over z_lo, x, y), col: 4 (over z_hi, core).
Axes of the slice: x: 4, y: 4, z: 8 (z_hi: 2, z_lo: 4; z = z_hi * 4 + z_lo), core: 2. Of those that a mesh axis runs over, the one named last changes fastest.
Arguments:
- charges: float32 [131072], P(('row', 'col')), may hold values from -6 to 6
- fractions: float32 [3, 131072], P(None, ('row', 'col')), may hold values from 0 to 1
- base_cells: int32 [3, 131072], P(None, ('row', 'col')), may hold values from 0 to 511, as said below
- counts: int32 [256], P(('row', 'col')), may hold values from 256 to 512, as said below
- influence: float32 [384, 256, 512], P(None, 'row', 'col'), as said below
Outputs:
- grad_charges: float32 [131072], P(('row', 'col'))
- grad_coords: float32 [3, 131072], P(None, ('row', 'col'))
Inputs may be any that keep to these rules, and one draw needn't show every extreme that they name: Atom slot i lies on device i // 512, numbered row index times the size of col plus col index; on the device with row index r and col index c, base_cells[0] lies in [r * 6, (r + 1) * 6), base_cells[1] in [c * 64, (c + 1) * 64), base_cells[2] anywhere. `counts`: slots from a device's count up to 512 hold no atom; some device is full in every draw. `influence`: nonnegative, zero at the zero wave vector.
All inputs are finite; a program needn't handle non-finite values.
Results may differ from a plain program's by a relative error of at most 0.0003.
Values sent between devices are 32-bit elements; how exact they have to be, the bound alone decides.
A program may use at most 64 MiB of HBM per device.

v0:
```python
import math

import jax
import jax.numpy as jnp
from jax import lax
from jax.sharding import PartitionSpec as P

KX = 384
KY = 256
KZ = 512
ORDER = 6


def from_behind(value, axis, steps):
    count = lax.axis_size(axis)
    pairs = [(source, (source + steps) % count) for source in range(count)]
    return lax.ppermute(value, axis, pairs)


def spline_tables(fraction):
    previous = [fraction, 1.0 - fraction]
    fifth_order = previous
    for degree in range(3, 7):
        current = []
        for position in range(degree):
            summed = jnp.zeros_like(fraction)
            if position < degree - 1:
                summed = (fraction + position) * previous[position]
            if position >= 1:
                summed = summed + (degree - fraction - position) * previous[position - 1]
            current.append(summed / (degree - 1))
        fifth_order = previous
        previous = current
    slopes = []
    for position in range(6):
        gradient = jnp.zeros_like(fraction)
        if position < 5:
            gradient = fifth_order[position]
        if position >= 1:
            gradient = gradient - fifth_order[position - 1]
        slopes.append(gradient)
    return (jnp.stack(previous[::-1]), jnp.stack(slopes[::-1]))


def cas_table(length):
    index = jnp.arange(length, dtype=jnp.int32)
    product = index[:, None] * index[None, :] % length
    angles = product.astype(jnp.float32) * (2.0 * math.pi / length)
    return jnp.cos(angles) + jnp.sin(angles)


def hartley_last(field, table):
    return jnp.einsum("xyz,zk->xyk", field, table, precision=lax.Precision.HIGHEST)


def hartley_middle(field, table):
    return jnp.einsum("xyz,yk->xkz", field, table, precision=lax.Precision.HIGHEST)


def hartley_first(field, table):
    return jnp.einsum("xyz,xk->kyz", field, table, precision=lax.Precision.HIGHEST)


def fold_middle(field, number_parts, rim_width):
    blocks = field.reshape(
        field.shape[0], number_parts, field.shape[1] // number_parts, field.shape[2]
    )
    inside = blocks.shape[2] - rim_width
    main_part = blocks[:, :, :inside]
    tail_part = jnp.roll(blocks[:, :, inside:], 1, axis=1)
    main_part = main_part.at[:, :, :rim_width].add(tail_part)
    return main_part.reshape(field.shape[0], number_parts * inside, field.shape[2])


def extend_middle(field, number_parts, rim_width):
    blocks = field.reshape(
        field.shape[0], number_parts, field.shape[1] // number_parts, field.shape[2]
    )
    tail_part = jnp.roll(blocks[:, :, :rim_width], -1, axis=1)
    joined = jnp.concatenate([blocks, tail_part], axis=2)
    return joined.reshape(field.shape[0], number_parts * joined.shape[2], field.shape[2])


def per_device(charges, fractions, base_cells, counts, influence):
    rows_count = lax.axis_size("row")
    cols_count = lax.axis_size("col")
    row_at = lax.axis_index("row")
    col_at = lax.axis_index("col")
    rim_width = ORDER - 1
    block_x = KX // rows_count
    block_y = KY // cols_count
    extent_x = block_x + rim_width
    extent_y = block_y + rim_width
    table_x = cas_table(KX)
    table_y = cas_table(KY)
    table_z = cas_table(KZ)
    slots = charges.shape[0]
    live_slot = jnp.arange(slots, dtype=jnp.int32) < counts[0]
    weight = jnp.where(live_slot, charges, jnp.float32(0.0))
    spline, spline_slope = spline_tables(fractions)
    offsets = jnp.arange(ORDER, dtype=jnp.int32)
    cell_x = base_cells[0][None, :] - row_at * block_x + offsets[:, None]
    cell_y = base_cells[1][None, :] - col_at * block_y + offsets[:, None]
    cell_z = (base_cells[2][None, :] + offsets[:, None]) % KZ
    cell_index = (cell_x[:, None, None, :] * extent_y + cell_y[None, :, None, :]) * KZ + cell_z[
        None, None, :, :
    ]
    values = (
        weight
        * spline[:, 0][:, None, None, :]
        * spline[:, 1][None, :, None, :]
        * spline[:, 2][None, None, :, :]
    )
    spread = jnp.zeros((extent_x * extent_y * KZ,), jnp.float32)
    spread = (
        spread.at[cell_index.reshape(-1)].add(values.reshape(-1)).reshape(extent_x, extent_y, KZ)
    )
    lower_rim = from_behind(spread[block_x:], "row", 1)
    spread = spread[:block_x].at[:rim_width].add(lower_rim)
    along_y = hartley_middle(
        fold_middle(
            lax.all_to_all(
                hartley_last(spread, table_z), "col", split_axis=2, concat_axis=1, tiled=True
            ),
            cols_count,
            rim_width,
        ),
        table_y,
    )
    spectrum = hartley_first(
        lax.all_to_all(along_y, "row", split_axis=1, concat_axis=0, tiled=True), table_x
    )
    returned = hartley_first(influence * spectrum, table_x)
    along_cols = extend_middle(
        hartley_middle(
            lax.all_to_all(returned, "row", split_axis=0, concat_axis=1, tiled=True), table_y
        ),
        cols_count,
        rim_width,
    )
    potential = hartley_last(
        lax.all_to_all(along_cols, "col", split_axis=1, concat_axis=2, tiled=True), table_z
    )
    upper_rows = from_behind(potential[:rim_width], "row", -1)
    potential = jnp.concatenate([potential, upper_rows], axis=0)
    patches = potential.reshape(-1)[cell_index]
    high = lax.Precision.HIGHEST
    grad_charge = jnp.einsum(
        "abcs,as,bs,cs->s", patches, spline[:, 0], spline[:, 1], spline[:, 2], precision=high
    )
    grad_first = jnp.einsum(
        "abcs,as,bs,cs->s", patches, spline_slope[:, 0], spline[:, 1], spline[:, 2], precision=high
    )
    grad_second = jnp.einsum(
        "abcs,as,bs,cs->s", patches, spline[:, 0], spline_slope[:, 1], spline[:, 2], precision=high
    )
    grad_third = jnp.einsum(
        "abcs,as,bs,cs->s", patches, spline[:, 0], spline[:, 1], spline_slope[:, 2], precision=high
    )
    grad_charges = jnp.where(live_slot, grad_charge, jnp.float32(0.0))
    grad_coords = weight[None, :] * jnp.stack([grad_first, grad_second, grad_third])
    return (grad_charges, grad_coords)


def solution(mesh):
    return jax.shard_map(
        per_device,
        mesh=mesh,
        in_specs=(
            P(("row", "col")),
            P(None, ("row", "col")),
            P(None, ("row", "col")),
            P(("row", "col")),
            P(None, "row", "col"),
        ),
        out_specs=(P(("row", "col")), P(None, ("row", "col"))),
        check_vma=False,
    )
```

profile of v0, /device:TPU:1, one launch (start us, length us, event | category | flops | bytes accessed | tf_op | source)
XLA Modules:
  0.0 1397.3 jit_solution(4547942115701411575)
XLA Ops:
  3.9 576.0 %scatter_custom_fusion = f32[388608]{0:T(1024)S(1)} fusion(s32[110592]{0:T(1024)S(1)} %bitcast.158, f32[110592]{0:T(1024)S(1)} %reshape.285, f32[]{:T(128)} %constant.180.clone.1), kind=kCustom, calls=%fused_computation.24 | custom fusion | flops 110592 | bytes 1554436 | tf_op jit(solution)/shard_map/scatter-add | solution.py:116
  579.9 1.0 slice.165
  580.9 2.1 collective-permute-start
  583.1 1.1 slice.162
  584.3 22.4 %collective-permute-done = f32[5,69,512]{2,1,0:T(8,128)} collective-permute-done((f32[5,69,512]{2,1,0:T(8,128)}, f32[5,69,512]{2,1,0:T(8,128)}, u32[]{:S(2)}, u32[]{:S(2)}) %collective-permute-start) | collective-permute-done | bytes 706592 | tf_op jit(solution)/shard_map/ppermute | solution.py:17
  606.7 2.1 add_dynamic-update-slice_fusion
  608.8 7.5 fusion.5
  617.1 2.0 reshape.313
  619.1 31.0 %all_to_all.69 = f32[4,1,52992]{2,1,0:T(1,128)S(1)} all-to-all(f32[4,1,52992]{2,1,0:T(1,128)S(1)} %reshape.313), channel_id=1, replica_groups=mesh['row'=64,'col'=4] {'col'}, dimensions={0} | all-to-all | bytes 1695744 | tf_op jit(solution)/shard_map/all_to_all | solution.py:122
  650.6 3.1 reduce.18
  653.7 1.5 reshape.314
  656.1 1.9 convolution_bitcast_fusion
  658.5 32.5 %all_to_all.70 = f32[6,256,128]{2,0,1:T(8,128)S(1)} all-to-all(f32[6,256,128]{2,0,1:T(8,128)S(1)} %copy.90), channel_id=1, replica_groups=mesh['row'=64,'col'=4] {'row'}, dimensions={1} | all-to-all | bytes 1572864 | tf_op jit(solution)/shard_map/all_to_all | solution.py:131
  691.2 3.8 convolution_multiply_fusion
  695.0 3.8 fusion.15
  699.4 27.4 %all_to_all.71 = f32[384,4,128]{2,1,0:T(4,128)S(1)} all-to-all(f32[384,4,128]{2,1,0:T(4,128)S(1)} %copy.94), channel_id=1, replica_groups=mesh['row'=64,'col'=4] {'row'}, dimensions={0} | all-to-all | bytes 1572864 | tf_op jit(solution)/shard_map/all_to_all | solution.py:136
  726.9 1.9 fusion.34
  728.9 1.5 copy.141
  730.4 6.4 all-to-all-start.3
  737.0 23.1 %all-to-all-done.3 = f32[6,276,128]{2,0,1:T(8,128)S(1)} async-done(((f32[6,276,128]{2,0,1:T(8,128)}), f32[6,276,128]{2,0,1:T(8,128)S(1)}, u32[]{:S(2)}, u32[]{:S(2)}) %all-to-all-start.3) | async-done | bytes 847904 | tf_op jit(solution)/shard_map/all_to_all | solution.py:142
  760.6 6.3 fusion.3
  771.8 9.3 collective-permute-done.1
  781.1 1.3 pad_maximum_fusion
  782.5 612.0 %gather_fusion = f32[110592]{0:T(1024)S(1)} fusion(f32[388608]{0:T(1024)S(1)} %reshape.272, s32[110592]{0:T(1024)} %broadcast_clamp_fusion), kind=kCustom, calls=%fused_computation | custom fusion | bytes 1327104 | tf_op jit(solution)/shard_map/gather | solution.py:146
  (88 shorter events, 14.4 us)
Async XLA Ops:
  0.6 2.0 copy-start.2
  1.5 2.1 copy-start.8
  3.7 576.2 %copy-start.6 = (f32[512]{0:T(512)}, f32[512]{0:T(512)S(1)}, u32[]{:S(2)}) copy-start(f32[512]{0:T(512)S(1)} %fusion.56) | copy-start | bytes 6148
  580.9 25.8 %collective-permute-start = (f32[5,69,512]{2,1,0:T(8,128)}, f32[5,69,512]{2,1,0:T(8,128)}, u32[]{:S(2)}, u32[]{:S(2)}) collective-permute-start(f32[5,69,512]{2,1,0:T(8,128)} %slice.165), channel_id=1, source_target_pairs={{0,4},{4,8},{8,12},{12,16},{16,20},{20,24},{24,28},{28,32},{32,36}... | collective-permute-start | bytes 2119688 | tf_op jit(solution)/shard_map/ppermute | solution.py:17
  658.5 32.7 %copy-start.9 = (f32[384,4,128]{2,1,0:T(4,128)S(1)}, f32[384,4,128]{2,1,0:T(4,128)}, u32[]{:S(2)}) copy-start(f32[384,4,128]{2,1,0:T(4,128)} %param.13) | copy-start | bytes 2359300
  730.4 29.6 %all-to-all-start.3 = ((f32[6,276,128]{2,0,1:T(8,128)}), f32[6,276,128]{2,0,1:T(8,128)S(1)}, u32[]{:S(2)}, u32[]{:S(2)}) async-start(f32[6,276,128]{2,0,1:T(8,128)} %bitcast.37), calls=%async_computation.3 | async-start | bytes 2260992 | tf_op jit(solution)/shard_map/all_to_all | solution.py:142
  767.0 14.1 %collective-permute-start.1 = (f32[5,69,512]{2,1,0:T(8,128)S(1)}, f32[5,69,512]{2,1,0:T(8,128)}, u32[]{:S(2)}, u32[]{:S(2)}) collective-permute-start(f32[5,69,512]{2,1,0:T(8,128)S(1)} %slice.190), channel_id=1, source_target_pairs={{0,252},{4,0},{8,4},{12,8},{16,12},{20,16},{24,20},{28,24},{32,28}... | collective-permute-start | bytes 2119688 | tf_op jit(solution)/shard_map/ppermute | solution.py:17
  782.5 612.1 %copy-start.3 = (f32[512,6,6]{0,2,1:T(8,128)S(1)}, f32[512,6,6]{0,2,1:T(8,128)}, u32[]{:S(2)}) copy-start(f32[512,6,6]{0,2,1:T(8,128)} %copy.151) | copy-start | bytes 221188
  782.5 612.1 %copy-start.4 = (f32[512,6,6]{0,2,1:T(8,128)S(1)}, f32[512,6,6]{0,2,1:T(8,128)}, u32[]{:S(2)}) copy-start(f32[512,6,6]{0,2,1:T(8,128)} %copy.152) | copy-start | bytes 221188
  782.5 612.1 %copy-start.5 = (f32[512,6,6]{0,2,1:T(8,128)S(1)}, f32[512,6,6]{0,2,1:T(8,128)}, u32[]{:S(2)}) copy-start(f32[512,6,6]{0,2,1:T(8,128)} %copy.150) | copy-start | bytes 221188
  1394.5 1.0 copy-start
  1394.5 1.0 copy-start.1
  1394.6 1.8 copy-start.7
where the time goes:
time: 1420 us; the launch traced here: 1400 us
  local copies, waits for them, and re-layouts  629 us (44%)
  other arithmetic  587 us (41%)
  blocking collectives  90.8 us (6%)
  waiting for transfers between devices  54.8 us (4%)
  matrix products  25.3 us (2%)
    gather x2, local copies, waits for them, and re-layouts, per_device(): patches = potential.reshape(-1)[cell_index]  612 us
    scatter-add x1, other arithmetic, per_device(): spread.at[cell_index.reshape(-1)].add(values.reshape(-1))  576 us
    all_to_all x1, blocking collectives, per_device(): lax.all_to_all(along_y, 'row', split_axis=1, concat_axis=0, tiled=True)  32.5 us
    ppermute x2, waiting for transfers between devices, from_behind(): return lax.ppermute(value, axis, pairs)  31.7 us
    all_to_all x1, blocking collectives, per_device(): lax.all_to_all(hartley_last(spread, table_z), 'col', split_axis=2, concat...  31 us
  transfers between devices with their start and end apart: 3, of which 3 were waited for; matrix products, arithmetic and copies ran while one was open for 0% of the time, Pallas kernels for 0%

commit v1 on v0

v1 whole, which is shorter than its diff:
```python
import functools
import math

import jax
import jax.numpy as jnp
import ml_dtypes
import numpy as np
from jax import lax
from jax.experimental import pallas as pl
from jax.experimental.pallas import tpu as pltpu
from jax.sharding import PartitionSpec as P

KX = 384
KY = 256
KZ = 512
ORDER = 6
SLOTS = 512
ROWS = 64
COLS = 4
CX = KX // ROWS
CY = KY // COLS
CZ = KZ // COLS
PATCH_Y = 72
FINE = 8
COARSE = KZ // FINE
FAN = 2 * FINE
VMEM_LIMIT = 50 * 1024 * 1024

HIGH_TYPE = jnp.bfloat16
FLOAT = jnp.float32


def split_table(table):
    high = table.astype(np.float32).astype(ml_dtypes.bfloat16)
    low = (table - high.astype(np.float64)).astype(np.float32).astype(ml_dtypes.bfloat16)
    return high, low


def cas(product, length):
    angles = (product % length) * (2.0 * math.pi / length)
    return np.cos(angles) + np.sin(angles)


def make_tables():
    kx = np.arange(KX)
    table_x = np.stack(split_table(cas(kx[:, None] * kx[None, :], KX)))
    ky = np.arange(KY)
    y = np.arange(KY + 8)
    table_y = np.stack(split_table(cas(y[:, None] * ky[None, :], KY)))
    kz = np.arange(KZ)
    coarse = (kz[:, None] * np.arange(COARSE)[None, :] * FINE % KZ) * (2.0 * math.pi / KZ)
    fine = kz[:, None] * np.arange(FAN)[None, :]
    table_z = np.zeros((COLS, 4 * CZ, 3 * FAN + 2 * COARSE), ml_dtypes.bfloat16)
    for place, values in ((0, np.cos(coarse)), (1, np.sin(coarse))):
        high, low = split_table(values)
        rows = slice(place * CZ, (place + 1) * CZ)
        table_z[:, rows, 3 * FAN : 3 * FAN + COARSE] = high.reshape(COLS, CZ, COARSE)
        table_z[:, rows, 3 * FAN + COARSE :] = low.reshape(COLS, CZ, COARSE)
    for place, values in ((2, cas(fine, KZ)), (3, cas(-fine, KZ))):
        high, low = split_table(values)
        rows = slice(place * CZ, (place + 1) * CZ)
        table_z[:, rows, :FAN] = high.reshape(COLS, CZ, FAN)
        table_z[:, rows, FAN : 2 * FAN] = high.reshape(COLS, CZ, FAN)
        table_z[:, rows, 2 * FAN : 3 * FAN] = low.reshape(COLS, CZ, FAN)
    return table_x, table_y, table_z


def spline_tables(fraction):
    previous = [fraction, 1.0 - fraction]
    fifth_order = previous
    for degree in range(3, 7):
        current = []
        for position in range(degree):
            summed = None
            if position < degree - 1:
                summed = (fraction + position) * previous[position]
            if position >= 1:
                second = (degree - fraction - position) * previous[position - 1]
                summed = second if summed is None else summed + second
            current.append(summed * (1.0 / (degree - 1)))
        fifth_order = previous
        previous = current
    slopes = []
    for position in range(6):
        if position == 0:
            slopes.append(fifth_order[0])
        elif position == 5:
            slopes.append(-fifth_order[4])
        else:
            slopes.append(fifth_order[position] - fifth_order[position - 1])
    return previous[::-1], slopes[::-1]


def split(value):
    high = value.astype(HIGH_TYPE)
    return high, (value - high.astype(FLOAT)).astype(HIGH_TYPE)


def dot(left, right, transposed=False):
    dims = (((1,), (1 if transposed else 0,)), ((), ()))
    return lax.dot_general(left, right, dims, preferred_element_type=FLOAT)


def dot3(left_high, left_low, right_high, right_low):
    return (
        dot(left_high, right_high) + dot(left_high, right_low) + dot(left_low, right_high)
    )


def dense(base, weights, rows):
    distance = lax.broadcasted_iota(jnp.int32, (rows, SLOTS), 0).astype(FLOAT) - base
    total = jnp.zeros((rows, SLOTS), FLOAT)
    for offset in range(ORDER):
        total = jnp.where(distance == offset, weights[offset], total)
    return total


def spread_kernel(atoms_ref, table_z_ref, table_y_ref, out_ref, z_ref, spline_ref, acc_ref):
    col = lax.axis_index("col")
    for dim in range(3):
        values, slopes = spline_tables(atoms_ref[:, 1 + dim, :])
        for offset in range(ORDER):
            spline_ref[dim, offset] = values[offset]
            spline_ref[dim, ORDER + offset] = slopes[offset]
    acc_ref[...] = jnp.zeros(acc_ref.shape, FLOAT)

    def block(index, carry):
        part = lax.rem(index, COLS)
        weight = atoms_ref[index, 0:1, :]
        base_x = atoms_ref[index, 4:5, :]
        base_y = atoms_ref[index, 5:6, :]
        base_z = atoms_ref[index, 6:7, :]

        def row(dim, place):
            return spline_ref[dim, place, pl.ds(index, 1), :]

        dense_x = weight * dense(base_x, [row(0, a) for a in range(ORDER)], 8)
        dense_y = dense(base_y, [row(1, a) for a in range(ORDER)], PATCH_Y)
        coarse = jnp.floor(base_z * (1.0 / FINE))
        rest = base_z - coarse * FINE
        hit = lax.broadcasted_iota(jnp.int32, (COARSE, SLOTS), 0).astype(FLOAT) == coarse
        hit = jnp.where(hit, 1.0, 0.0).astype(HIGH_TYPE)
        fine_high, fine_low = split(dense(rest, [row(2, a) for a in range(ORDER)], FAN))
        slope_high, slope_low = split(dense(rest, [row(2, ORDER + a) for a in range(ORDER)], FAN))
        table = table_z_ref[col]
        joined = jnp.concatenate([fine_high, fine_low, fine_high, hit, hit], axis=0)
        parts = dot(table, joined)
        joined_slope = jnp.concatenate([slope_high, slope_low, slope_high], axis=0)
        parts_slope = dot(table[2 * CZ :, : 3 * FAN], joined_slope)
        cosine, sine = parts[:CZ], parts[CZ : 2 * CZ]
        wave = cosine * parts[2 * CZ : 3 * CZ] + sine * parts[3 * CZ :]
        wave_slope = cosine * parts_slope[:CZ] + sine * parts_slope[CZ:]
        wave_high, wave_low = split(wave)
        slope_high, slope_low = split(wave_slope)
        z_ref[index, 0:CZ] = wave_high
        z_ref[index, CZ : 2 * CZ] = wave_low
        z_ref[index, 2 * CZ : 3 * CZ] = slope_high
        z_ref[index, 3 * CZ :] = slope_low
        patch = jnp.concatenate([dense_x[x : x + 1] * dense_y for x in range(CX)], axis=0)
        patch_high, patch_low = split(patch)
        first = dot(patch_high, jnp.concatenate([wave_high, wave_low], axis=0), True)
        summed = first[:, :CZ] + first[:, CZ:] + dot(patch_low, wave_high, True)
        rows = pl.ds(pl.multiple_of(part * CY, CY), PATCH_Y)
        for x in range(CX):
            acc_ref[x, rows, :] += summed[x * PATCH_Y : (x + 1) * PATCH_Y]
        return carry

    lax.fori_loop(0, 2 * COLS, block, 0)
    for x in range(CX):
        acc_ref[x, 0:8, :] += acc_ref[x, KY : KY + 8, :]
    for pair in range(CX // 2):
        field = jnp.concatenate([acc_ref[2 * pair, :KY], acc_ref[2 * pair + 1, :KY]], axis=1)
        high, low = split(field)
        result = dot3(table_y_ref[0, :KY], table_y_ref[1, :KY], high, low)
        out_ref[2 * pair] = result[:, :CZ]
        out_ref[2 * pair + 1] = result[:, CZ:]


def middle_kernel(field_ref, influence_ref, table_ref, out_ref):
    width = KY // ROWS
    field = jnp.concatenate([field_ref[pl.ds(j, KX, stride=width), :] for j in range(width)], axis=1)
    weight = jnp.concatenate(
        [influence_ref[pl.ds(j, KX, stride=width), :] for j in range(width)], axis=1
    )
    high, low = split(field)
    spectrum = weight * dot3(table_ref[0], table_ref[1], high, low)
    high, low = split(spectrum)
    result = dot3(table_ref[0], table_ref[1], high, low)
    for j in range(width):
        out_ref[pl.ds(j, KX, stride=width), :] = result[:, j * CZ : (j + 1) * CZ]


def gather_kernel(field_ref, atoms_ref, z_ref, spline_ref, table_y_ref, out_ref, real_ref):
    for pair in range(CX // 2):
        field = jnp.concatenate([field_ref[2 * pair], field_ref[2 * pair + 1]], axis=1)
        high, low = split(field)
        result = dot3(table_y_ref[0], table_y_ref[1], high, low)
        real_ref[2 * pair] = result[:, :CZ]
        real_ref[2 * pair + 1] = result[:, CZ:]

    def block(index, carry):
        part = lax.rem(index, COLS)
        base_x = atoms_ref[index, 4:5, :]
        base_y = atoms_ref[index, 5:6, :]

        def row(dim, place):
            return spline_ref[dim, place, pl.ds(index, 1), :]

        dense_x = dense(base_x, [row(0, a) for a in range(ORDER)], 8)
        slope_x = dense(base_x, [row(0, ORDER + a) for a in range(ORDER)], 8)
        dense_y = dense(base_y, [row(1, a) for a in range(ORDER)], PATCH_Y)
        slope_y = dense(base_y, [row(1, ORDER + a) for a in range(ORDER)], PATCH_Y)
        rows = pl.ds(pl.multiple_of(part * CY, CY), PATCH_Y)
        patch = jnp.concatenate([real_ref[x, rows, :] for x in range(CX)], axis=0)
        high, low = split(patch)
        both = jnp.concatenate([high, low], axis=1)

        def contract(place):
            wave_high = z_ref[index, place * CZ : (place + 1) * CZ]
            wave_low = z_ref[index, (place + 1) * CZ : (place + 2) * CZ]
            return dot(both, jnp.concatenate([wave_high, wave_high], axis=0)) + dot(high, wave_low)

        plain = contract(0)
        third = contract(2)
        charge = first = second = last = 0.0
        for x in range(CX):
            here = plain[x * PATCH_Y : (x + 1) * PATCH_Y]
            there = third[x * PATCH_Y : (x + 1) * PATCH_Y]
            inner = jnp.sum(dense_y * here, axis=0, keepdims=True)
            along_y = jnp.sum(slope_y * here, axis=0, keepdims=True)
            along_z = jnp.sum(dense_y * there, axis=0, keepdims=True)
            charge = charge + dense_x[x : x + 1] * inner
            first = first + slope_x[x : x + 1] * inner
            second = second + dense_x[x : x + 1] * along_y
            last = last + dense_x[x : x + 1] * along_z
        out_ref[index, 0:1] = charge
        out_ref[index, 1:2] = first
        out_ref[index, 2:3] = second
        out_ref[index, 3:4] = last
        return carry

    lax.fori_loop(0, 2 * COLS, block, 0)


def call(kernel, outs, scratch=()):
    return pl.pallas_call(
        kernel,
        out_shape=outs,
        scratch_shapes=list(scratch),
        compiler_params=pltpu.CompilerParams(vmem_limit_bytes=VMEM_LIMIT),
    )


def shape(dims, kind=FLOAT):
    return jax.ShapeDtypeStruct(dims, kind)


def per_device(charges, fractions, base_cells, counts, influence):
    table_x, table_y, table_z = (jnp.asarray(t) for t in make_tables())
    row_at = lax.axis_index("row")
    col_at = lax.axis_index("col")
    live_slot = jnp.arange(SLOTS, dtype=jnp.int32) < counts[0]
    weight = jnp.where(live_slot, charges, jnp.float32(0.0))
    offsets = jnp.stack([row_at * CX, col_at * CY, jnp.zeros((), jnp.int32)])
    local = (base_cells - offsets[:, None]).astype(FLOAT)
    pack = jnp.concatenate(
        [weight[None], fractions, local, jnp.zeros((1, SLOTS), FLOAT)], axis=0
    )
    shared = lax.all_gather(pack, "col")
    forward = [(source, (source + 1) % ROWS) for source in range(ROWS)]
    behind = lax.ppermute(shared, "row", forward)
    behind = behind.at[:, 4].add(-float(CX))
    atoms = jnp.concatenate([shared, behind], axis=0)
    blocks = 2 * COLS
    spectrum, waves, splines = call(
        spread_kernel,
        (
            shape((CX, KY, CZ)),
            shape((blocks, 4 * CZ, SLOTS), HIGH_TYPE),
            shape((3, 2 * ORDER, blocks, SLOTS)),
        ),
        [pltpu.VMEM((CX, KY + 8, CZ), FLOAT)],
    )(atoms, table_z, table_y)
    turned = lax.all_to_all(spectrum, "row", split_axis=1, concat_axis=0, tiled=True)
    width = KY // ROWS
    field = call(middle_kernel, shape((KX * width, CZ)))(
        turned.reshape(KX * width, CZ), influence.reshape(KX * width, CZ), table_x
    )
    returned = lax.all_to_all(
        field.reshape(KX, width, CZ), "row", split_axis=0, concat_axis=1, tiled=True
    )
    partial = call(
        gather_kernel,
        shape((blocks, 4, SLOTS)),
        [pltpu.VMEM((CX, KY + 8, CZ), FLOAT)],
    )(returned, atoms, waves, splines, table_y)
    backward = [(source, (source - 1) % ROWS) for source in range(ROWS)]
    mine = partial[:COLS] + lax.ppermute(partial[COLS:], "row", backward)
    total = lax.psum_scatter(mine, "col", scatter_dimension=0, tiled=False)
    grad_charges = jnp.where(live_slot, total[0], jnp.float32(0.0))
    grad_coords = weight[None, :] * total[1:]
    return (grad_charges, grad_coords)


def solution(mesh):
    return jax.shard_map(
        per_device,
        mesh=mesh,
        in_specs=(
            P(("row", "col")),
            P(None, ("row", "col")),
            P(None, ("row", "col")),
            P(("row", "col")),
            P(None, "row", "col"),
        ),
        out_specs=(P(("row", "col")), P(None, ("row", "col"))),
        check_vma=False,
    )
```

time: 1420 us -> 133 us (0.09); the launches traced: 1400 us -> 132 us
  local copies, waits for them, and re-layouts: 629 us -> 4.39 us
  other arithmetic: 587 us -> 4.16 us
  waiting for transfers between devices: 54.8 us -> 9.17 us
  matrix products: 25.3 us -> 0 us
  Pallas kernels: 0 us -> 17.7 us
    gather x2 -> x0, local copies, waits for them, and re-layouts: 612 us -> none  [per_device(): patches = potential.reshape(-1)[cell_index]]
    scatter-add x3 -> x0, other arithmetic: 578 us -> none  [the longest x1 576 us: per_device(): spread.at[cell_index.reshape(-1)].add(values.reshape(-1))]
    all_to_all x3 -> x2, blocking collectives: 90.8 us -> 58.4 us  [the longest x1 31.1 us: per_device(): lax.all_to_all(spectrum, 'row', split_axis=1, concat_axis=0, tiled=True)]
    dot_general x6 -> x0, matrix products: 25.3 us -> none  [the longest x2 13.8 us: hartley_last(): jnp.einsum('xyz,zk->xyk', field, table, precision=lax.Precision.HIGHEST)]
    all_to_all x1 -> x0, waiting for transfers between devices: 23.1 us -> none  [per_device(): lax.all_to_all(along_cols, 'col', split_axis=1, concat_axis=2, tiled=True)]
    ppermute x2, waiting for transfers between devices: 31.7 us -> 9.17 us  [the longest x1 8.73 us: per_device(): behind = lax.ppermute(shared, 'row', forward)]
    unnamed x0 -> x1, blocking collectives: none -> 20.3 us
    pallas_call x0 -> x3, Pallas kernels: none -> 17.7 us  [the longest x1 8.23 us: per_device(): call(spread_kernel, (shape((CX, KY, CZ)), shape((blocks, 4 * CZ, SLOTS),...]
  transfers between devices with their start and end apart: 3 -> 2, of which waited for: 3 -> 2; matrix products, arithmetic and copies ran while one was open for 0% -> 0% of each run, Pallas kernels for 0% -> 0%
where the time goes in v1:
time: 133 us; the launch traced here: 132 us
  blocking collectives  91 us (68%)
  Pallas kernels  17.7 us (13%)
  waiting for transfers between devices  9.17 us (7%)
  local copies, waits for them, and re-layouts  4.39 us (3%)
  other arithmetic  4.16 us (3%)
  starting transfers between devices  3.92 us (3%)
  between operations  1.39 us (1%)
    all_to_all x1, blocking collectives, per_device(): lax.all_to_all(spectrum, 'row', split_axis=1, concat_axis=0, tiled=True)  31.1 us
    all_to_all x1, blocking collectives, per_device(): lax.all_to_all(field.reshape(KX, width, CZ), 'row', split_axis=0, concat_...  27.4 us
    unnamed x1, blocking collectives  20.3 us
    all_gather x1, blocking collectives, per_device(): shared = lax.all_gather(pack, 'col')  12.2 us
    ppermute x1, waiting for transfers between devices, per_device(): behind = lax.ppermute(shared, 'row', forward)  8.73 us
    pallas_call x1, Pallas kernels, per_device(): call(spread_kernel, (shape((CX, KY, CZ)), shape((blocks, 4 * CZ, SLOTS),...  8.23 us
    pallas_call x1, Pallas kernels, per_device(): call(gather_kernel, shape((blocks, 4, SLOTS)), [pltpu.VMEM((CX, KY + 8, C...  7.94 us
    ppermute x1, starting transfers between devices, per_device(): mine = partial[:COLS] + lax.ppermute(partial[COLS:], 'row', backward)  3.1 us
  transfers between devices with their start and end apart: 2, of which 2 were waited for; matrix products, arithmetic and copies ran while one was open for 0% of the time, Pallas kernels for 0%

profile of v1, /device:TPU:1, one launch (start us, length us, event | category | flops | bytes accessed | tf_op | source)
XLA Modules:
  0.0 131.7 jit_solution(11656233451902303770)
XLA Ops:
  1.4 0.8 subtract_convert_fusion
  2.1 0.7 fusion.2
  2.9 0.8 maximum_maximum_fusion
  3.7 12.2 %all-gather = f32[32,512]{1,0:T(8,128)S(1)} all-gather(f32[8,512]{1,0:T(8,128)S(1)} %maximum_maximum_fusion), channel_id=2, replica_groups=mesh['row'=64,'col'=4] {'col'}, dimensions={0}, use_global_device_ids=true | all-gather | bytes 81920 | tf_op jit(solution)/shard_map/all_gather | solution.py:269
  15.9 0.8 collective-permute-start
  16.7 8.7 %collective-permute-done = f32[4,8,512]{2,1,0:T(8,128)S(1)} collective-permute-done((f32[4,8,512]{2,1,0:T(8,128)S(1)}, f32[4,8,512]{2,1,0:T(8,128)S(1)}, u32[]{:S(2)}, u32[]{:S(2)}) %collective-permute-start) | collective-permute-done | bytes 65568 | tf_op jit(solution)/shard_map/ppermute | solution.py:271
  25.4 0.1 scatter-add.4
  25.5 0.9 copy-done
  26.5 1.2 copy-done.2
  27.7 8.2 %shard_map.95 = (f32[6,256,128]{2,1,0:T(8,128)S(1)}, bf16[8,512,512]{2,1,0:T(8,128)(2,1)}, f32[3,12,8,512]{3,2,1,0:T(8,128)S(1)}) custom-call(f32[8,8,512]{2,1,0:T(8,128)S(1)} %pad_maximum_fusion.atoms_ref, bf16[4,512,176]{2,1,0:T(8,128)(2,1)S(1)} %copy-done.2, bf16[2,264,256]{2,1,0:T(8,128)(2,1)S(1)} %copy-done), custom_call_target="tpu_custom_call" | custom-call | tf_op jit(solution)/shard_map/pallas_call | solution.py:275
  35.9 0.5 copy.13
  36.4 31.1 %all_to_all.33 = f32[6,256,128]{2,0,1:T(8,128)S(1)} all-to-all(f32[6,256,128]{2,0,1:T(8,128)S(1)} %copy.13), channel_id=1, replica_groups=mesh['row'=64,'col'=4] {'row'}, dimensions={1} | all-to-all | bytes 1572864 | tf_op jit(solution)/shard_map/all_to_all | solution.py:284
  67.5 0.2 copy.14
  67.7 1.5 %shard_map.96 = f32[1536,128]{1,0:T(8,128)S(1)} custom-call(f32[1536,128]{1,0:T(8,128)S(1)} %bitcast.24, f32[1536,128]{1,0:T(8,128)S(1)} %bitcast.27, bf16[2,384,384]{2,1,0:T(8,128)(2,1)S(1)} %copy-done.4), custom_call_target="tpu_custom_call" | custom-call | tf_op jit(solution)/shard_map/pallas_call | solution.py:286
  69.2 27.4 %all_to_all.34 = f32[384,4,128]{2,1,0:T(4,128)S(1)} all-to-all(f32[384,4,128]{2,1,0:T(4,128)S(1)} %bitcast.25), channel_id=1, replica_groups=mesh['row'=64,'col'=4] {'row'}, dimensions={0} | all-to-all | bytes 1572864 | tf_op jit(solution)/shard_map/all_to_all | solution.py:289
  96.6 0.1 copy.15
  96.8 7.9 %shard_map.97 = f32[8,4,512]{2,1,0:T(4,128)S(1)} custom-call(f32[6,256,128]{2,1,0:T(8,128)S(1)} %bitcast.26, f32[8,8,512]{2,1,0:T(8,128)S(1)} %pad_maximum_fusion.atoms_ref, bf16[8,512,512]{2,1,0:T(8,128)(2,1)} %get-tuple-element.18.z_ref, f32[3,12,8,512]{3,2,1,0:T(8,128)S(1)} %get-tuple-element.19.spline_ref, bf16[2,264,256]{2,1,0:T(8,128)(2,1)S(1)} %copy-done.1), custom_call_target="tpu_custom_call" | custom-call | tf_op jit(solution)/shard_map/pallas_call | solution.py:292
  104.7 3.1 %collective-permute-start.1 = (f32[4,4,512]{2,1,0:T(4,128)S(1)}, f32[4,4,512]{2,1,0:T(4,128)S(1)}, u32[]{:S(2)}, u32[]{:S(2)}) collective-permute-start(f32[4,4,512]{2,1,0:T(4,128)S(1)} %slice.46), channel_id=1, source_target_pairs={{0,252},{4,0},{8,4},{12,8},{16,12},{20,16},{24,20},{28,24},{32,28}... | collective-permute-start | bytes 98312 | tf_op jit(solution)/shard_map/ppermute | solution.py:298
  107.8 0.6 dynamic-slice.7
  108.4 0.4 collective-permute-done.1
  108.9 20.3 %all-reduce = f32[4,4,512]{2,1,0:T(4,128)S(1)} all-reduce(f32[4,4,512]{2,1,0:T(4,128)S(1)} %slice_add_fusion), channel_id=3, replica_groups=mesh['row'=64,'col'=4] {'col'}, use_global_device_ids=true, to_apply=%region_0.1.clone | all-reduce | flops 8192 | bytes 65536
  129.2 0.6 constant_dynamic-slice_fusion
  129.8 1.3 fusion
  131.1 0.6 fusion.1
  (16 shorter events, 0.2 us)
Async XLA Ops:
  15.9 9.5 %collective-permute-start = (f32[4,8,512]{2,1,0:T(8,128)S(1)}, f32[4,8,512]{2,1,0:T(8,128)S(1)}, u32[]{:S(2)}, u32[]{:S(2)}) collective-permute-start(f32[4,8,512]{2,1,0:T(8,128)S(1)} %bitcast.30), channel_id=1, source_target_pairs={{0,4},{4,8},{8,12},{12,16},{16,20},{20,24},{24,28},{28,32},{32,36}... | collective-permute-start | bytes 196616 | tf_op jit(solution)/shard_map/ppermute | solution.py:271
  25.5 1.0 copy-start
  26.5 1.2 copy-start.2
  27.7 40.0 %copy-start.3 = (f32[384,4,128]{2,1,0:T(4,128)S(1)}, f32[384,4,128]{2,1,0:T(4,128)}, u32[]{:S(2)}) copy-start(f32[384,4,128]{2,1,0:T(4,128)} %param.14) | copy-start | bytes 2359300
  27.7 40.0 %copy-start.4 = (bf16[2,384,384]{2,1,0:T(8,128)(2,1)S(1)}, bf16[2,384,384]{2,1,0:T(8,128)(2,1)}, u32[]{:S(2)}) copy-start(bf16[2,384,384]{2,1,0:T(8,128)(2,1)} %constant.55.clone.table_ref) | copy-start | bytes 1769476
  67.5 29.3 %copy-start.1 = (bf16[2,264,256]{2,1,0:T(8,128)(2,1)S(1)}, bf16[2,264,256]{2,1,0:T(8,128)(2,1)}, u32[]{:S(2)}) copy-start(bf16[2,264,256]{2,1,0:T(8,128)(2,1)} %constant.56.clone.table_y_ref) | copy-start | bytes 811012
  96.6 11.2 %copy-start.5 = (u32[256]{0:T(256)S(1)}, u32[256]{0:T(256)}, u32[]{:S(2)}) copy-start(u32[256]{0:T(256)} %constant.62) | copy-start | bytes 3076
  104.7 4.1 %collective-permute-start.1 = (f32[4,4,512]{2,1,0:T(4,128)S(1)}, f32[4,4,512]{2,1,0:T(4,128)S(1)}, u32[]{:S(2)}, u32[]{:S(2)}) collective-permute-start(f32[4,4,512]{2,1,0:T(4,128)S(1)} %slice.46), channel_id=1, source_target_pairs={{0,252},{4,0},{8,4},{12,8},{16,12},{20,16},{24,20},{28,24},{32,28}... | collective-permute-start | bytes 98312 | tf_op jit(solution)/shard_map/ppermute | solution.py:298

commit v2 on v1

v2 whole, which is shorter than its diff:
```python
import math

import jax
import jax.numpy as jnp
import ml_dtypes
import numpy as np
from jax import lax
from jax.experimental import pallas as pl
from jax.experimental.pallas import tpu as pltpu
from jax.sharding import PartitionSpec as P

KX = 384
KY = 256
KZ = 512
ORDER = 6
SLOTS = 512
ROWS = 64
COLS = 4
CX = KX // ROWS
CY = KY // COLS
CZ = KZ // COLS
PATCH_Y = 72
FINE = 8
COARSE = KZ // FINE
FAN = 2 * FINE
VMEM_LIMIT = 50 * 1024 * 1024
SPREAD_GROUPS = 3
GATHER_GROUPS = 3
MESH = pl.DeviceIdType.MESH

HIGH_TYPE = jnp.bfloat16
FLOAT = jnp.float32


def split_table(table):
    high = table.astype(np.float32).astype(ml_dtypes.bfloat16)
    low = (table - high.astype(np.float64)).astype(np.float32).astype(ml_dtypes.bfloat16)
    return high, low


def cas(product, length):
    angles = (product % length) * (2.0 * math.pi / length)
    return np.cos(angles) + np.sin(angles)


def make_tables():
    kx = np.arange(KX)
    table_x = np.stack(split_table(cas(kx[:, None] * kx[None, :], KX)))
    ky = np.arange(KY)
    y = np.arange(KY + 8)
    table_y = np.stack(split_table(cas(y[:, None] * ky[None, :], KY)))
    kz = np.arange(KZ)
    coarse = (kz[:, None] * np.arange(COARSE)[None, :] * FINE % KZ) * (2.0 * math.pi / KZ)
    fine = kz[:, None] * np.arange(FAN)[None, :]
    table_z = np.zeros((COLS, 4 * CZ, 3 * FAN + 2 * COARSE), ml_dtypes.bfloat16)
    for place, values in ((0, np.cos(coarse)), (1, np.sin(coarse))):
        high, low = split_table(values)
        rows = slice(place * CZ, (place + 1) * CZ)
        table_z[:, rows, 3 * FAN : 3 * FAN + COARSE] = high.reshape(COLS, CZ, COARSE)
        table_z[:, rows, 3 * FAN + COARSE :] = low.reshape(COLS, CZ, COARSE)
    for place, values in ((2, cas(fine, KZ)), (3, cas(-fine, KZ))):
        high, low = split_table(values)
        rows = slice(place * CZ, (place + 1) * CZ)
        table_z[:, rows, :FAN] = high.reshape(COLS, CZ, FAN)
        table_z[:, rows, FAN : 2 * FAN] = high.reshape(COLS, CZ, FAN)
        table_z[:, rows, 2 * FAN : 3 * FAN] = low.reshape(COLS, CZ, FAN)
    return table_x, table_y, table_z


def spline_tables(fraction):
    previous = [fraction, 1.0 - fraction]
    fifth_order = previous
    for degree in range(3, 7):
        current = []
        for position in range(degree):
            summed = None
            if position < degree - 1:
                summed = (fraction + position) * previous[position]
            if position >= 1:
                second = (degree - fraction - position) * previous[position - 1]
                summed = second if summed is None else summed + second
            current.append(summed * (1.0 / (degree - 1)))
        fifth_order = previous
        previous = current
    slopes = []
    for position in range(6):
        if position == 0:
            slopes.append(fifth_order[0])
        elif position == 5:
            slopes.append(-fifth_order[4])
        else:
            slopes.append(fifth_order[position] - fifth_order[position - 1])
    return previous[::-1], slopes[::-1]


def split(value):
    high = value.astype(HIGH_TYPE)
    return high, (value - high.astype(FLOAT)).astype(HIGH_TYPE)


def dot(left, right, transposed=False):
    dims = (((1,), (1 if transposed else 0,)), ((), ()))
    return lax.dot_general(left, right, dims, preferred_element_type=FLOAT)


def dot3(left_high, left_low, right_high, right_low):
    return (
        dot(left_high, right_high) + dot(left_high, right_low) + dot(left_low, right_high)
    )


def dense(base, weights, rows):
    distance = lax.broadcasted_iota(jnp.int32, (rows, SLOTS), 0).astype(FLOAT) - base
    total = jnp.zeros((rows, SLOTS), FLOAT)
    for offset in range(ORDER):
        total = jnp.where(distance == offset, weights[offset], total)
    return total


def kernel(
    charges_ref,
    fractions_ref,
    cells_ref,
    counts_ref,
    influence_hbm,
    table_x_hbm,
    table_y_hbm,
    table_z_hbm,
    out_charges_ref,
    out_coords_ref,
    influence_ref,
    table_x_ref,
    table_y_ref,
    table_z_ref,
    atoms_ref,
    spline_ref,
    dense_x_ref,
    dense_y_ref,
    z_ref,
    acc_ref,
    send_ref,
    turned_ref,
    back_ref,
    returned_ref,
    partial_ref,
    arrived_ref,
    local_sems,
    send_sems,
    atoms_sem,
    turned_sem,
    returned_sems,
    arrived_sem,
):
    row = lax.axis_index("row")
    col = lax.axis_index("col")
    row_after = lax.rem(row + 1, ROWS)
    row_before = lax.rem(row + ROWS - 1, ROWS)
    width = KY // ROWS
    blocks = 2 * COLS

    barrier = pltpu.get_barrier_semaphore()

    def greet(device_row, device_col):
        pl.semaphore_signal(
            barrier, inc=1, device_id=(device_row, device_col), device_id_type=MESH
        )

    for step in range(1, COLS):
        other = lax.rem(col + step, COLS)
        greet(row, other)
        greet(row_after, other)
        greet(row_before, other)

    @pl.loop(1, ROWS)
    def _(step):
        greet(lax.rem(row + step, ROWS), col)

    fetches = [
        pltpu.make_async_copy(table_z_hbm.at[col], table_z_ref, local_sems.at[0]),
        pltpu.make_async_copy(table_y_hbm, table_y_ref, local_sems.at[1]),
        pltpu.make_async_copy(table_x_hbm, table_x_ref, local_sems.at[2]),
        pltpu.make_async_copy(influence_hbm, influence_ref, local_sems.at[3]),
    ]
    for fetch in fetches:
        fetch.start()

    slot = lax.broadcasted_iota(jnp.int32, (1, SLOTS), 1)
    live = slot < counts_ref[0]
    weight = jnp.where(live, charges_ref[...], 0.0)
    atoms_ref[col, 0:1, :] = weight
    atoms_ref[col, 1:4, :] = fractions_ref[...]
    cells = cells_ref[...]
    atoms_ref[col, 4:5, :] = (cells[0:1] - row * CX).astype(FLOAT)
    atoms_ref[col, 5:6, :] = (cells[1:2] - col * CY).astype(FLOAT)
    atoms_ref[col, 6:7, :] = cells[2:3].astype(FLOAT)
    atoms_ref[col, 7:8, :] = weight

    pl.semaphore_wait(barrier, ROWS - 1 + 3 * (COLS - 1))

    def remote(source, target, send_sem, recv_sem, device_row, device_col):
        return pltpu.make_async_remote_copy(
            src_ref=source,
            dst_ref=target,
            send_sem=send_sem,
            recv_sem=recv_sem,
            device_id=(device_row, device_col),
            device_id_type=MESH,
        )

    for step in range(1, COLS):
        other = lax.rem(col + step, COLS)
        remote(
            atoms_ref.at[col], atoms_ref.at[col], send_sems.at[0], atoms_sem, row, other
        ).start()
    for step in range(COLS):
        other = lax.rem(col + step, COLS)
        remote(
            atoms_ref.at[col],
            atoms_ref.at[COLS + col],
            send_sems.at[0],
            atoms_sem,
            row_after,
            other,
        ).start()
    remote(
        atoms_ref.at[0 : blocks - 1],
        atoms_ref.at[0 : blocks - 1],
        send_sems.at[0],
        atoms_sem,
        row_after,
        col,
    ).wait()

    for dim in range(3):
        values, slopes = spline_tables(atoms_ref[:, 1 + dim, :])
        for offset in range(ORDER):
            spline_ref[dim, offset] = values[offset]
            spline_ref[dim, ORDER + offset] = slopes[offset]
    fetches[0].wait()

    @pl.loop(0, blocks)
    def _(index):
        shift = (CX * (index // COLS)).astype(FLOAT)
        weight = atoms_ref[index, 0:1, :]
        base_x = atoms_ref[index, 4:5, :] - shift
        base_y = atoms_ref[index, 5:6, :]
        base_z = atoms_ref[index, 6:7, :]

        def rows(dim, place):
            return [
                spline_ref[dim, place + offset, pl.ds(index, 1), :] for offset in range(ORDER)
            ]

        plain_x = dense(base_x, rows(0, 0), 8)
        dense_x_ref[index, 0] = plain_x
        dense_x_ref[index, 1] = dense(base_x, rows(0, ORDER), 8)
        dense_x_ref[index, 2] = weight * plain_x
        dense_y_ref[index, 0] = dense(base_y, rows(1, 0), PATCH_Y)
        dense_y_ref[index, 1] = dense(base_y, rows(1, ORDER), PATCH_Y)
        coarse = jnp.floor(base_z * (1.0 / FINE))
        rest = base_z - coarse * FINE
        hit = lax.broadcasted_iota(jnp.int32, (COARSE, SLOTS), 0).astype(FLOAT) == coarse
        hit = jnp.where(hit, 1.0, 0.0).astype(HIGH_TYPE)
        fine_high, fine_low = split(dense(rest, rows(2, 0), FAN))
        slope_high, slope_low = split(dense(rest, rows(2, ORDER), FAN))
        joined = jnp.concatenate([fine_high, fine_low, fine_high, hit, hit], axis=0)
        parts = dot(table_z_ref[...], joined)
        joined_slope = jnp.concatenate([slope_high, slope_low, slope_high], axis=0)
        parts_slope = dot(table_z_ref[2 * CZ :, : 3 * FAN], joined_slope)
        cosine, sine = parts[:CZ], parts[CZ : 2 * CZ]
        wave = cosine * parts[2 * CZ : 3 * CZ] + sine * parts[3 * CZ :]
        wave_slope = cosine * parts_slope[:CZ] + sine * parts_slope[CZ:]
        wave_high, wave_low = split(wave)
        slope_high, slope_low = split(wave_slope)
        z_ref[index, 0:CZ] = wave_high
        z_ref[index, CZ : 2 * CZ] = wave_low
        z_ref[index, 2 * CZ : 3 * CZ] = slope_high
        z_ref[index, 3 * CZ :] = slope_low

    send_flat = send_ref.reshape(CX, KY, CZ)
    for group in range(SPREAD_GROUPS):
        count = CX // SPREAD_GROUPS
        first_x = group * count
        acc_ref[0:count] = jnp.zeros((count, KY + 8, CZ), FLOAT)

        @pl.loop(0, blocks)
        def _(index):
            part = lax.rem(index, COLS)
            plain_y = dense_y_ref[index, 0]
            patch = jnp.concatenate(
                [dense_x_ref[index, 2, x : x + 1, :] * plain_y for x in range(first_x, first_x + count)],
                axis=0,
            )
            high, low = split(patch)
            both = dot(high, z_ref[index, 0 : 2 * CZ], True)
            summed = both[:, :CZ] + both[:, CZ:] + dot(low, z_ref[index, 0:CZ], True)
            rows = pl.ds(pl.multiple_of(part * CY, CY), PATCH_Y)
            for x in range(count):
                acc_ref[x, rows, :] += summed[x * PATCH_Y : (x + 1) * PATCH_Y]

        if group == 0:
            fetches[1].wait()
        for x in range(count):
            acc_ref[x, 0:8, :] += acc_ref[x, KY : KY + 8, :]
        field = jnp.concatenate([acc_ref[x, :KY] for x in range(count)], axis=1)
        high, low = split(field)
        result = dot3(table_y_ref[0, :KY], table_y_ref[1, :KY], high, low)
        for x in range(count):
            send_flat[first_x + x] = result[:, x * CZ : (x + 1) * CZ]
        places = pl.ds(first_x, count)

        @pl.loop(1, ROWS)
        def _(step):
            target = lax.rem(row + step, ROWS)
            remote(
                send_ref.at[places, target],
                turned_ref.at[row, places],
                send_sems.at[1],
                turned_sem,
                target,
                col,
            ).start()

    turned_ref[row] = send_ref[:, row]
    fetches[2].wait()
    fetches[3].wait()
    influence = jnp.concatenate(
        [influence_ref[pl.ds(j, KX, stride=width), :] for j in range(width)], axis=1
    )
    remote(
        turned_ref.at[0 : ROWS - 1],
        turned_ref.at[0 : ROWS - 1],
        send_sems.at[1],
        turned_sem,
        row_after,
        col,
    ).wait()

    turned_flat = turned_ref.reshape(KX * width, CZ)
    field = jnp.concatenate(
        [turned_flat[pl.ds(j, KX, stride=width), :] for j in range(width)], axis=1
    )
    high, low = split(field)
    spectrum = influence * dot3(table_x_ref[0], table_x_ref[1], high, low)
    high, low = split(spectrum)
    result = dot3(table_x_ref[0], table_x_ref[1], high, low)
    back_flat = back_ref.reshape(KX * width, CZ)
    for j in range(width):
        back_flat[pl.ds(j, KX, stride=width), :] = result[:, j * CZ : (j + 1) * CZ]

    count = CX // GATHER_GROUPS
    for group in range(GATHER_GROUPS):
        places = pl.ds(group * count, count)

        @pl.loop(1, ROWS)
        def _(step):
            target = lax.rem(row + step, ROWS)
            remote(
                back_ref.at[target, places],
                returned_ref.at[places, row],
                send_sems.at[2],
                returned_sems.at[group],
                target,
                col,
            ).start()

    returned_ref[:, row] = back_ref[row]

    returned_flat = returned_ref.reshape(CX, KY, CZ)
    for group in range(GATHER_GROUPS):
        places = slice(group * count, (group + 1) * count)
        remote(
            returned_ref.at[places, 0 : ROWS - 1],
            returned_ref.at[places, 0 : ROWS - 1],
            send_sems.at[2],
            returned_sems.at[group],
            row_after,
            col,
        ).wait_recv()
        field = jnp.concatenate(
            [returned_flat[group * count + x] for x in range(count)], axis=1
        )
        high, low = split(field)
        result = dot3(table_y_ref[0], table_y_ref[1], high, low)
        for x in range(count):
            acc_ref[x] = result[:, x * CZ : (x + 1) * CZ]

        @pl.loop(1, blocks + 1)
        def _(step):
            index = lax.rem(col + step, blocks)
            part = lax.rem(index, COLS)
            plain_y = dense_y_ref[index, 0]
            slope_y = dense_y_ref[index, 1]
            rows = pl.ds(pl.multiple_of(part * CY, CY), PATCH_Y)
            patch = jnp.concatenate([acc_ref[x, rows, :] for x in range(count)], axis=0)
            high, low = split(patch)
            both = jnp.concatenate([high, low], axis=1)

            def contract(place):
                wave_high = z_ref[index, place * CZ : (place + 1) * CZ]
                wave_low = z_ref[index, (place + 1) * CZ : (place + 2) * CZ]
                twice = jnp.concatenate([wave_high, wave_high], axis=0)
                return dot(both, twice) + dot(high, wave_low)

            plain = contract(0)
            third = contract(2)
            if group == 0:
                sums = [0.0] * 4
            else:
                sums = [partial_ref[index, k : k + 1] for k in range(4)]
            for x in range(count):
                here = plain[x * PATCH_Y : (x + 1) * PATCH_Y]
                there = third[x * PATCH_Y : (x + 1) * PATCH_Y]
                inner = jnp.sum(plain_y * here, axis=0, keepdims=True)
                along_y = jnp.sum(slope_y * here, axis=0, keepdims=True)
                along_z = jnp.sum(plain_y * there, axis=0, keepdims=True)
                place = group * count + x
                plain_x = dense_x_ref[index, 0, place : place + 1, :]
                slope_x = dense_x_ref[index, 1, place : place + 1, :]
                sums[0] = sums[0] + plain_x * inner
                sums[1] = sums[1] + slope_x * inner
                sums[2] = sums[2] + plain_x * along_y
                sums[3] = sums[3] + plain_x * along_z
            for k in range(4):
                partial_ref[index, k : k + 1] = sums[k]
            if group == GATHER_GROUPS - 1:
                behind = index // COLS

                @pl.when(step < blocks)
                def _():
                    remote(
                        partial_ref.at[index],
                        arrived_ref.at[behind * COLS + col],
                        send_sems.at[3],
                        arrived_sem,
                        lax.rem(row + ROWS - behind, ROWS),
                        part,
                    ).start()

    arrived_ref[col] = partial_ref[col]
    remote(
        arrived_ref.at[0 : blocks - 1],
        arrived_ref.at[0 : blocks - 1],
        send_sems.at[3],
        arrived_sem,
        row_after,
        col,
    ).wait()
    total = arrived_ref[0]
    for index in range(1, blocks):
        total = total + arrived_ref[index]
    out_charges_ref[...] = jnp.where(live, total[0:1], 0.0)
    out_coords_ref[...] = atoms_ref[col, 7:8, :] * total[1:4]
    remote(
        returned_ref.at[:, 0 : ROWS - 1],
        returned_ref.at[:, 0 : ROWS - 1],
        send_sems.at[2],
        returned_sems.at[0],
        row_after,
        col,
    ).wait_send()


def shape(dims, kind=FLOAT):
    return jax.ShapeDtypeStruct(dims, kind)


def per_device(charges, fractions, base_cells, counts, influence):
    tables = [jnp.asarray(t) for t in make_tables()]
    width = KY // ROWS
    blocks = 2 * COLS
    anywhere = pl.BlockSpec(memory_space=pltpu.HBM)
    vector = pl.BlockSpec(memory_space=pltpu.VMEM)
    dma = pltpu.SemaphoreType.DMA
    grad_charges, grad_coords = pl.pallas_call(
        kernel,
        out_shape=(shape((1, SLOTS)), shape((3, SLOTS))),
        in_specs=[vector, vector, vector, pl.BlockSpec(memory_space=pltpu.SMEM)] + [anywhere] * 4,
        out_specs=(vector, vector),
        scratch_shapes=[
            pltpu.VMEM((KX * width, CZ), FLOAT),
            pltpu.VMEM(tables[0].shape, HIGH_TYPE),
            pltpu.VMEM(tables[1].shape, HIGH_TYPE),
            pltpu.VMEM(tables[2].shape[1:], HIGH_TYPE),
            pltpu.VMEM((blocks, 8, SLOTS), FLOAT),
            pltpu.VMEM((3, 2 * ORDER, blocks, SLOTS), FLOAT),
            pltpu.VMEM((blocks, 3, 8, SLOTS), FLOAT),
            pltpu.VMEM((blocks, 2, PATCH_Y, SLOTS), FLOAT),
            pltpu.VMEM((blocks, 4 * CZ, SLOTS), HIGH_TYPE),
            pltpu.VMEM((CX, KY + 8, CZ), FLOAT),
            pltpu.VMEM((CX, ROWS, width, CZ), FLOAT),
            pltpu.VMEM((ROWS, CX, width, CZ), FLOAT),
            pltpu.VMEM((ROWS, CX, width, CZ), FLOAT),
            pltpu.VMEM((CX, ROWS, width, CZ), FLOAT),
            pltpu.VMEM((blocks, 4, SLOTS), FLOAT),
            pltpu.VMEM((blocks, 4, SLOTS), FLOAT),
            dma((4,)),
            dma((4,)),
            dma,
            dma,
            dma((GATHER_GROUPS,)),
            dma,
        ],
        compiler_params=pltpu.CompilerParams(
            collective_id=0, has_side_effects=True, vmem_limit_bytes=VMEM_LIMIT
        ),
    )(
        charges.reshape(1, SLOTS),
        fractions,
        base_cells,
        counts,
        influence.reshape(KX * width, CZ),
        *tables,
    )
    return grad_charges.reshape(SLOTS), grad_coords


def solution(mesh):
    return jax.shard_map(
        per_device,
        mesh=mesh,
        in_specs=(
            P(("row", "col")),
            P(None, ("row", "col")),
            P(None, ("row", "col")),
            P(("row", "col")),
            P(None, "row", "col"),
        ),
        out_specs=(P(("row", "col")), P(None, ("row", "col"))),
        check_vma=False,
    )
```

time: 133 us -> 83.8 us (0.63)
  blocking collectives: 91 us -> 0 us
  Pallas kernels: 17.7 us -> 74.5 us
  waiting for transfers between devices: 9.17 us -> 0 us
  other arithmetic: 4.16 us -> 0 us
  starting transfers between devices: 3.92 us -> 0 us
  local copies, waits for them, and re-layouts: 4.39 us -> 7.62 us
    all_to_all x2 -> x0, blocking collectives: 58.4 us -> none  [the longest x1 31.1 us: per_device(): lax.all_to_all(spectrum, 'row', split_axis=1, concat_axis=0, tiled=True)]
    pallas_call x3 -> x1, Pallas kernels: 17.7 us -> 74.5 us  [per_device(): pl.pallas_call(kernel, out_shape=(shape((1, SLOTS)), shape((3, SLOTS))),...]
    unnamed x1 -> x0, blocking collectives: 20.3 us -> none
    all_gather x1 -> x0, blocking collectives: 12.2 us -> none  [per_device(): shared = lax.all_gather(pack, 'col')]
    ppermute x2 -> x0, waiting for transfers between devices: 9.17 us -> none  [the longest x1 8.73 us: per_device(): behind = lax.ppermute(shared, 'row', forward)]
    unnamed x13 -> x16, local copies, waits for them, and re-layouts: 2.77 us -> 7.62 us
    ppermute x2 -> x0, starting transfers between devices: 3.92 us -> none  [the longest x1 3.1 us: per_device(): mine = partial[:COLS] + lax.ppermute(partial[COLS:], 'row', backward)]
  transfers between devices with their start and end apart: 2 -> 0, of which waited for: 2 -> 0; matrix products, arithmetic and copies ran while one was open for 0% -> 0% of each run, Pallas kernels for 0% -> 0%
where the time goes in v2:
time: 83.8 us; the launch traced here: 83.4 us
  Pallas kernels  74.5 us (89%)
  local copies, waits for them, and re-layouts  7.62 us (9%)
  between operations  1.3 us (2%)
    pallas_call x1, Pallas kernels, per_device(): pl.pallas_call(kernel, out_shape=(shape((1, SLOTS)), shape((3, SLOTS))),...  74.5 us
    unnamed x16, local copies, waits for them, and re-layouts  7.62 us

profile of v2, /device:TPU:1, one launch (start us, length us, event | category | flops | bytes accessed | tf_op | source)
XLA Modules:
  0.0 83.4 jit_solution(10267689685640786809)
XLA Ops:
  1.3 0.0 copy-start.6
  1.3 0.7 copy-done.6
  2.0 0.0 copy-start
  2.0 1.2 %copy-done = bf16[4,512,176]{2,1,0:T(8,128)(2,1)S(1)} copy-done((bf16[4,512,176]{2,1,0:T(8,128)(2,1)S(1)}, bf16[4,512,176]{2,1,0:T(8,128)(2,1)}, u32[]{:S(2)}) %copy-start) | copy-done | bytes 720920
  3.2 0.0 copy-start.1
  3.2 1.1 %copy-done.1 = f32[384,4,128]{2,1,0:T(4,128)S(1)} copy-done((f32[384,4,128]{2,1,0:T(4,128)S(1)}, f32[384,4,128]{2,1,0:T(4,128)}, u32[]{:S(2)}) %copy-start.1) | copy-done | bytes 786456
  4.3 0.0 copy-start.2
  4.3 1.1 %copy-done.2 = bf16[2,384,384]{2,1,0:T(8,128)(2,1)S(1)} copy-done((bf16[2,384,384]{2,1,0:T(8,128)(2,1)S(1)}, bf16[2,384,384]{2,1,0:T(8,128)(2,1)}, u32[]{:S(2)}) %copy-start.2) | copy-done | bytes 589848
  5.4 0.0 copy-start.3
  5.4 1.0 %copy-done.3 = bf16[2,264,256]{2,1,0:T(8,128)(2,1)S(1)} copy-done((bf16[2,264,256]{2,1,0:T(8,128)(2,1)S(1)}, bf16[2,264,256]{2,1,0:T(8,128)(2,1)}, u32[]{:S(2)}) %copy-start.3) | copy-done | bytes 270360
  6.3 0.0 copy-start.4
  6.3 0.7 copy-done.4
  7.0 0.0 copy-start.5
  7.0 0.7 copy-done.5
  7.7 74.5 %shard_map.95 = (f32[1,512]{1,0:T(1,128)S(1)}, f32[3,512]{1,0:T(4,128)S(1)}) custom-call(f32[1,512]{1,0:T(1,128)S(1)} %bitcast.4, f32[3,512]{1,0:T(4,128)S(1)} %copy-done.4, s32[3,512]{1,0:T(4,128)S(1)} %copy-done.5, s32[1]{0:T(128)S(6)} %copy.12.counts_ref, f32[1536,128]{1,0:T(8,128)S(1)} %bitcast.3, bf16[2,384,384]{2,1,0:T(8,128)(2,1)S(1)} %copy-done.2, ...), custom_call_target="tpu_custom_call" | custom-call | tf_op jit(solution)/shard_map/pallas_call | solution.py:475
  82.2 0.6 copy.13
  82.8 0.6 copy.14
Async XLA Ops:
  1.3 0.7 copy-start.6
  2.0 1.2 %copy-start = (bf16[4,512,176]{2,1,0:T(8,128)(2,1)S(1)}, bf16[4,512,176]{2,1,0:T(8,128)(2,1)}, u32[]{:S(2)}) copy-start(bf16[4,512,176]{2,1,0:T(8,128)(2,1)} %constant.8.clone.table_z_hbm) | copy-start | bytes 2162692
  3.2 1.1 %copy-start.1 = (f32[384,4,128]{2,1,0:T(4,128)S(1)}, f32[384,4,128]{2,1,0:T(4,128)}, u32[]{:S(2)}) copy-start(f32[384,4,128]{2,1,0:T(4,128)} %param.12) | copy-start | bytes 2359300
  4.3 1.1 %copy-start.2 = (bf16[2,384,384]{2,1,0:T(8,128)(2,1)S(1)}, bf16[2,384,384]{2,1,0:T(8,128)(2,1)}, u32[]{:S(2)}) copy-start(bf16[2,384,384]{2,1,0:T(8,128)(2,1)} %constant.6.clone.table_x_hbm) | copy-start | bytes 1769476
  5.4 1.0 %copy-start.3 = (bf16[2,264,256]{2,1,0:T(8,128)(2,1)S(1)}, bf16[2,264,256]{2,1,0:T(8,128)(2,1)}, u32[]{:S(2)}) copy-start(bf16[2,264,256]{2,1,0:T(8,128)(2,1)} %constant.7.clone.table_y_hbm) | copy-start | bytes 811012
  6.3 0.7 copy-start.4
  7.0 0.7 copy-start.5

commit v3 on v2

--- a/solution.py
+++ b/solution.py
@@ -23,9 +23,10 @@
 FINE = 8
 COARSE = KZ // FINE
 FAN = 2 * FINE
-VMEM_LIMIT = 50 * 1024 * 1024
-SPREAD_GROUPS = 3
-GATHER_GROUPS = 3
+VMEM_LIMIT = 63 * 1024 * 1024
+UNROLL = 8
+SPREAD_GROUPS = 2
+GATHER_GROUPS = 2
 MESH = pl.DeviceIdType.MESH
 
 HIGH_TYPE = jnp.bfloat16
@@ -45,7 +46,8 @@
 
 def make_tables():
     kx = np.arange(KX)
-    table_x = np.stack(split_table(cas(kx[:, None] * kx[None, :], KX)))
+    table_x = np.zeros((2, KX + 8, KX), ml_dtypes.bfloat16)
+    table_x[:, :KX] = split_table(cas(kx[:, None] * kx[None, :], KX))
     ky = np.arange(KY)
     y = np.arange(KY + 8)
     table_y = np.stack(split_table(cas(y[:, None] * ky[None, :], KY)))
@@ -64,7 +66,7 @@
         table_z[:, rows, :FAN] = high.reshape(COLS, CZ, FAN)
         table_z[:, rows, FAN : 2 * FAN] = high.reshape(COLS, CZ, FAN)
         table_z[:, rows, 2 * FAN : 3 * FAN] = low.reshape(COLS, CZ, FAN)
-    return table_x, table_y, table_z
+    return table_x, table_y, np.pad(table_z, ((0, 0), (0, 8), (0, 0)))
 
 
 def spline_tables(fraction):
@@ -137,6 +139,7 @@
     dense_x_ref,
     dense_y_ref,
     z_ref,
+    turn_ref,
     acc_ref,
     send_ref,
     turned_ref,
@@ -238,7 +241,7 @@
             spline_ref[dim, ORDER + offset] = slopes[offset]
     fetches[0].wait()
 
-    @pl.loop(0, blocks)
+    @pl.loop(0, blocks, unroll=UNROLL)
     def _(index):
         shift = (CX * (index // COLS)).astype(FLOAT)
         weight = atoms_ref[index, 0:1, :]
@@ -251,31 +254,22 @@
                 spline_ref[dim, place + offset, pl.ds(index, 1), :] for offset in range(ORDER)
             ]
 
-        plain_x = dense(base_x, rows(0, 0), 8)
-        dense_x_ref[index, 0] = plain_x
-        dense_x_ref[index, 1] = dense(base_x, rows(0, ORDER), 8)
-        dense_x_ref[index, 2] = weight * plain_x
+        dense_x_ref[index, 2] = weight * dense(base_x, rows(0, 0), 8)
         dense_y_ref[index, 0] = dense(base_y, rows(1, 0), PATCH_Y)
-        dense_y_ref[index, 1] = dense(base_y, rows(1, ORDER), PATCH_Y)
         coarse = jnp.floor(base_z * (1.0 / FINE))
         rest = base_z - coarse * FINE
         hit = lax.broadcasted_iota(jnp.int32, (COARSE, SLOTS), 0).astype(FLOAT) == coarse
         hit = jnp.where(hit, 1.0, 0.0).astype(HIGH_TYPE)
         fine_high, fine_low = split(dense(rest, rows(2, 0), FAN))
-        slope_high, slope_low = split(dense(rest, rows(2, ORDER), FAN))
         joined = jnp.concatenate([fine_high, fine_low, fine_high, hit, hit], axis=0)
-        parts = dot(table_z_ref[...], joined)
-        joined_slope = jnp.concatenate([slope_high, slope_low, slope_high], axis=0)
-        parts_slope = dot(table_z_ref[2 * CZ :, : 3 * FAN], joined_slope)
+        parts = dot(table_z_ref[: 4 * CZ], joined)
         cosine, sine = parts[:CZ], parts[CZ : 2 * CZ]
+        turn_ref[index, :CZ] = cosine
+        turn_ref[index, CZ:] = sine
         wave = cosine * parts[2 * CZ : 3 * CZ] + sine * parts[3 * CZ :]
-        wave_slope = cosine * parts_slope[:CZ] + sine * parts_slope[CZ:]
         wave_high, wave_low = split(wave)
-        slope_high, slope_low = split(wave_slope)
         z_ref[index, 0:CZ] = wave_high
         z_ref[index, CZ : 2 * CZ] = wave_low
-        z_ref[index, 2 * CZ : 3 * CZ] = slope_high
-        z_ref[index, 3 * CZ :] = slope_low
 
     send_flat = send_ref.reshape(CX, KY, CZ)
     for group in range(SPREAD_GROUPS):
@@ -283,7 +277,7 @@
         first_x = group * count
         acc_ref[0:count] = jnp.zeros((count, KY + 8, CZ), FLOAT)
 
-        @pl.loop(0, blocks)
+        @pl.loop(0, blocks, unroll=UNROLL)
         def _(index):
             part = lax.rem(index, COLS)
             plain_y = dense_y_ref[index, 0]
@@ -320,6 +314,29 @@
                 target,
                 col,
             ).start()
+
+    @pl.loop(0, blocks, unroll=UNROLL)
+    def _(index):
+        base_x = atoms_ref[index, 4:5, :] - (CX * (index // COLS)).astype(FLOAT)
+        base_y = atoms_ref[index, 5:6, :]
+        base_z = atoms_ref[index, 6:7, :]
+
+        def rows(dim, place):
+            return [
+                spline_ref[dim, place + offset, pl.ds(index, 1), :] for offset in range(ORDER)
+            ]
+
+        dense_x_ref[index, 0] = dense(base_x, rows(0, 0), 8)
+        dense_x_ref[index, 1] = dense(base_x, rows(0, ORDER), 8)
+        dense_y_ref[index, 1] = dense(base_y, rows(1, ORDER), PATCH_Y)
+        rest = base_z - jnp.floor(base_z * (1.0 / FINE)) * FINE
+        high, low = split(dense(rest, rows(2, ORDER), FAN))
+        joined = jnp.concatenate([high, low, high], axis=0)
+        parts = dot(table_z_ref[2 * CZ : 4 * CZ, : 3 * FAN], joined)
+        wave = turn_ref[index, :CZ] * parts[:CZ] + turn_ref[index, CZ:] * parts[CZ:]
+        high, low = split(wave)
+        z_ref[index, 2 * CZ : 3 * CZ] = high
+        z_ref[index, 3 * CZ :] = low
 
     turned_ref[row] = send_ref[:, row]
     fetches[2].wait()
@@ -341,9 +358,9 @@
         [turned_flat[pl.ds(j, KX, stride=width), :] for j in range(width)], axis=1
     )
     high, low = split(field)
-    spectrum = influence * dot3(table_x_ref[0], table_x_ref[1], high, low)
+    spectrum = influence * dot3(table_x_ref[0, :KX], table_x_ref[1, :KX], high, low)
     high, low = split(spectrum)
-    result = dot3(table_x_ref[0], table_x_ref[1], high, low)
+    result = dot3(table_x_ref[0, :KX], table_x_ref[1, :KX], high, low)
     back_flat = back_ref.reshape(KX * width, CZ)
     for j in range(width):
         back_flat[pl.ds(j, KX, stride=width), :] = result[:, j * CZ : (j + 1) * CZ]
@@ -385,7 +402,7 @@
         for x in range(count):
             acc_ref[x] = result[:, x * CZ : (x + 1) * CZ]
 
-        @pl.loop(1, blocks + 1)
+        @pl.loop(1, blocks + 1, unroll=UNROLL)
         def _(step):
             index = lax.rem(col + step, blocks)
             part = lax.rem(index, COLS)
@@ -487,6 +504,7 @@
             pltpu.VMEM((blocks, 3, 8, SLOTS), FLOAT),
             pltpu.VMEM((blocks, 2, PATCH_Y, SLOTS), FLOAT),
             pltpu.VMEM((blocks, 4 * CZ, SLOTS), HIGH_TYPE),
+            pltpu.VMEM((blocks, 2 * CZ, SLOTS), FLOAT),
             pltpu.VMEM((CX, KY + 8, CZ), FLOAT),
             pltpu.VMEM((CX, ROWS, width, CZ), FLOAT),
             pltpu.VMEM((ROWS, CX, width, CZ), FLOAT),

time: 83.8 us -> 75.6 us (0.902)
  local copies, waits for them, and re-layouts: 7.62 us -> 2.53 us
  Pallas kernels: 74.5 us -> 70.7 us
    unnamed x16 -> x2, local copies, waits for them, and re-layouts: 7.62 us -> 2.53 us
    pallas_call x1, Pallas kernels: 74.5 us -> 70.7 us  [per_device(): pl.pallas_call(kernel, out_shape=(shape((1, SLOTS)), shape((3, SLOTS))),...]
where the time goes in v3:
time: 75.6 us; the launch traced here: 74.6 us
  Pallas kernels  70.7 us (94%)
  local copies, waits for them, and re-layouts  2.53 us (3%)
  between operations  1.29 us (2%)
    pallas_call x1, Pallas kernels, per_device(): pl.pallas_call(kernel, out_shape=(shape((1, SLOTS)), shape((3, SLOTS))),...  70.7 us
    unnamed x2, local copies, waits for them, and re-layouts  2.53 us

profile of v3, /device:TPU:1, one launch (start us, length us, event | category | flops | bytes accessed | tf_op | source)
XLA Modules:
  0.0 74.6 jit_solution(3767059906983053088)
XLA Ops:
  1.3 70.7 %shard_map.95 = (f32[1,512]{1,0:T(1,128)}, f32[3,512]{1,0:T(4,128)}) custom-call(f32[1,512]{1,0:T(1,128)} %bitcast.5, f32[3,512]{1,0:T(4,128)} %fractions_ref.1, s32[3,512]{1,0:T(4,128)} %cells_ref.1, s32[1]{0:T(128)S(6)} %copy.12.counts_ref, f32[1536,128]{1,0:T(8,128)} %bitcast.3, bf16[2,392,384]{2,1,0:T(8,128)(2,1)} %constant.6.clone.table_x_hbm, ...), custom_call_target="tpu_custom_call" | custom-call | tf_op jit(solution)/shard_map/pallas_call | solution.py:492
  72.0 1.2 %copy.13 = f32[512]{0:T(512)} copy(f32[512]{0:T(512)} %bitcast.4) | data formatting | bytes 4096
  73.3 1.3 %copy.14 = f32[3,512]{1,0:T(4,128)} copy(f32[3,512]{1,0:T(4,128)} %get-tuple-element.9) | data formatting | bytes 12288

commit v4 on v3

v4 whole, which is shorter than its diff:
```python
import math

import jax
import jax.numpy as jnp
import ml_dtypes
import numpy as np
from jax import lax
from jax.experimental import pallas as pl
from jax.experimental.pallas import tpu as pltpu
from jax.sharding import PartitionSpec as P

KX = 384
KY = 256
KZ = 512
ORDER = 6
SLOTS = 512
ROWS = 64
COLS = 4
CX = KX // ROWS
CY = KY // COLS
CZ = KZ // COLS
PATCH_Y = 72
FINE = 8
COARSE = KZ // FINE
FAN = 2 * FINE
VMEM_LIMIT = 63 * 1024 * 1024
GATHER_GROUPS = 1
HALVES = 2
WIDTH = KY // ROWS
PART = WIDTH // HALVES
BLOCKS = 2 * COLS
MESH = pl.DeviceIdType.MESH

HIGH_TYPE = jnp.bfloat16
FLOAT = jnp.float32


def split_table(table):
    high = table.astype(np.float32).astype(ml_dtypes.bfloat16)
    low = (table - high.astype(np.float64)).astype(np.float32).astype(ml_dtypes.bfloat16)
    return high, low


def cas(product, length):
    angles = (product % length) * (2.0 * math.pi / length)
    return np.cos(angles) + np.sin(angles)


def make_tables():
    kx = np.arange(KX)
    table_x = np.zeros((2, KX + 8, KX), ml_dtypes.bfloat16)
    table_x[:, :KX] = split_table(cas(kx[:, None] * kx[None, :], KX))
    ky = np.arange(KY).reshape(ROWS, HALVES, PART).transpose(1, 0, 2).reshape(KY)
    y = np.arange(KY + 8)
    table_y = np.stack(split_table(cas(ky[:, None] * np.arange(KY)[None, :], KY)))
    table_y = np.pad(table_y, ((0, 0), (0, 8), (0, 0)))
    table_back = np.stack(split_table(cas(y[:, None] * ky[None, :], KY)))
    kz = np.arange(KZ)
    coarse = (kz[:, None] * np.arange(COARSE)[None, :] * FINE % KZ) * (2.0 * math.pi / KZ)
    fine = kz[:, None] * np.arange(FAN)[None, :]
    table_z = np.zeros((COLS, 4 * CZ, 3 * FAN + 2 * COARSE), ml_dtypes.bfloat16)
    for place, values in ((0, np.cos(coarse)), (1, np.sin(coarse))):
        high, low = split_table(values)
        rows = slice(place * CZ, (place + 1) * CZ)
        table_z[:, rows, 3 * FAN : 3 * FAN + COARSE] = high.reshape(COLS, CZ, COARSE)
        table_z[:, rows, 3 * FAN + COARSE :] = low.reshape(COLS, CZ, COARSE)
    for place, values in ((2, cas(fine, KZ)), (3, cas(-fine, KZ))):
        high, low = split_table(values)
        rows = slice(place * CZ, (place + 1) * CZ)
        table_z[:, rows, :FAN] = high.reshape(COLS, CZ, FAN)
        table_z[:, rows, FAN : 2 * FAN] = high.reshape(COLS, CZ, FAN)
        table_z[:, rows, 2 * FAN : 3 * FAN] = low.reshape(COLS, CZ, FAN)
    return table_x, table_y, table_back, np.pad(table_z, ((0, 0), (0, 8), (0, 0)))


def spline_tables(fraction):
    previous = [fraction, 1.0 - fraction]
    fifth_order = previous
    for degree in range(3, 7):
        current = []
        for position in range(degree):
            summed = None
            if position < degree - 1:
                summed = (fraction + position) * previous[position]
            if position >= 1:
                second = (degree - fraction - position) * previous[position - 1]
                summed = second if summed is None else summed + second
            current.append(summed * (1.0 / (degree - 1)))
        fifth_order = previous
        previous = current
    slopes = []
    for position in range(6):
        if position == 0:
            slopes.append(fifth_order[0])
        elif position == 5:
            slopes.append(-fifth_order[4])
        else:
            slopes.append(fifth_order[position] - fifth_order[position - 1])
    return previous[::-1], slopes[::-1]


def split(value):
    high = value.astype(HIGH_TYPE)
    return high, (value - high.astype(FLOAT)).astype(HIGH_TYPE)


def dot(left, right, transposed=False):
    dims = (((1,), (1 if transposed else 0,)), ((), ()))
    return lax.dot_general(left, right, dims, preferred_element_type=FLOAT)


def dot3(left_high, left_low, right_high, right_low):
    return (
        dot(left_high, right_high) + dot(left_high, right_low) + dot(left_low, right_high)
    )


def dense(base, weights, rows):
    distance = lax.broadcasted_iota(jnp.int32, (rows, SLOTS), 0).astype(FLOAT) - base
    total = jnp.zeros((rows, SLOTS), FLOAT)
    for offset in range(ORDER):
        total = jnp.where(distance == offset, weights[offset], total)
    return total


def kernel(
    charges_ref,
    fractions_ref,
    cells_ref,
    counts_ref,
    influence_hbm,
    table_x_hbm,
    table_y_hbm,
    table_back_hbm,
    table_z_hbm,
    out_ref,
    influence_ref,
    table_x_ref,
    table_y_ref,
    table_back_ref,
    table_z_ref,
    atoms_ref,
    slope_ref,
    dense_x_ref,
    dense_y_ref,
    z_ref,
    turn_ref,
    acc_ref,
    send_ref,
    turned_ref,
    back_ref,
    returned_ref,
    partial_ref,
    arrived_ref,
    local_sems,
    send_sems,
    atoms_sems,
    turned_sems,
    returned_sems,
    arrived_sem,
):
    row = lax.axis_index("row")
    col = lax.axis_index("col")
    half_at = col // 2
    core = lax.rem(col, 2)
    row_after = lax.rem(row + 1, ROWS)
    row_before = lax.rem(row + ROWS - 1, ROWS)
    sibling = half_at * 2 + 1 - core
    far_cols = [(1 - half_at) * 2 + core, (1 - half_at) * 2 + 1 - core]

    barrier = pltpu.get_barrier_semaphore()

    def greet(device_row, device_col):
        pl.semaphore_signal(
            barrier, inc=1, device_id=(device_row, device_col), device_id_type=MESH
        )

    for other in far_cols + [sibling]:
        greet(row, other)
        greet(row_after, other)
        greet(row_before, other)

    @pl.loop(1, ROWS)
    def _(step):
        greet(lax.rem(row + step, ROWS), col)

    fetches = [
        pltpu.make_async_copy(table_z_hbm.at[col], table_z_ref, local_sems.at[0]),
        pltpu.make_async_copy(table_y_hbm, table_y_ref, local_sems.at[1]),
        pltpu.make_async_copy(table_x_hbm, table_x_ref, local_sems.at[2]),
        pltpu.make_async_copy(influence_hbm, influence_ref, local_sems.at[3]),
        pltpu.make_async_copy(table_back_hbm, table_back_ref, local_sems.at[4]),
    ]
    for fetch in fetches:
        fetch.start()

    slot = lax.broadcasted_iota(jnp.int32, (1, SLOTS), 1)
    weight = jnp.where(slot < counts_ref[0], charges_ref[...], 0.0)
    atoms_ref[col, 0:1, :] = weight
    atoms_ref[col, 1:4, :] = fractions_ref[...]
    cells = cells_ref[...]
    atoms_ref[col, 4:5, :] = (cells[0:1] - row * CX).astype(FLOAT)
    atoms_ref[col, 5:6, :] = (cells[1:2] - col * CY).astype(FLOAT)
    atoms_ref[col, 6:7, :] = cells[2:3].astype(FLOAT)
    atoms_ref[col, 7:8, :] = weight
    acc_ref[...] = jnp.zeros(acc_ref.shape, FLOAT)

    def remote(source, target, send_sem, recv_sem, device_row, device_col):
        return pltpu.make_async_remote_copy(
            src_ref=source,
            dst_ref=target,
            send_sem=send_sem,
            recv_sem=recv_sem,
            device_id=(device_row, device_col),
            device_id_type=MESH,
        )

    def bases(index, behind):
        base_x = atoms_ref[index, 4:5, :] + float(CX) * (-behind)
        base_z = atoms_ref[index, 6:7, :]
        coarse = jnp.floor(base_z * (1.0 / FINE))
        return base_x, atoms_ref[index, 5:6, :], coarse, base_z - coarse * FINE

    def prepare(index, behind):
        values, slopes = spline_tables(atoms_ref[index, 1:4, :])
        for offset in range(ORDER):
            slope_ref[index, offset, 0:3, :] = slopes[offset]
        base_x, base_y, coarse, rest = bases(index, behind)

        def rows(dim):
            return [value[dim : dim + 1] for value in values]

        plain_x = dense(base_x, rows(0), 8)
        dense_x_ref[index, 0] = plain_x
        dense_x_ref[index, 2] = atoms_ref[index, 0:1, :] * plain_x
        dense_y_ref[index, 0] = dense(base_y, rows(1), PATCH_Y)
        hit = lax.broadcasted_iota(jnp.int32, (COARSE, SLOTS), 0).astype(FLOAT) == coarse
        hit = jnp.where(hit, 1.0, 0.0).astype(HIGH_TYPE)
        fine_high, fine_low = split(dense(rest, rows(2), FAN))
        joined = jnp.concatenate([fine_high, fine_low, fine_high, hit, hit], axis=0)
        parts = dot(table_z_ref[: 4 * CZ], joined)
        cosine, sine = parts[:CZ], parts[CZ : 2 * CZ]
        turn_ref[index, :CZ] = cosine
        turn_ref[index, CZ:] = sine
        wave = cosine * parts[2 * CZ : 3 * CZ] + sine * parts[3 * CZ :]
        wave_high, wave_low = split(wave)
        z_ref[index, 0:CZ] = wave_high
        z_ref[index, CZ : 2 * CZ] = wave_low

    def prepare_slopes(index, behind):
        base_x, base_y, coarse, rest = bases(index, behind)

        def rows(dim):
            return [slope_ref[index, offset, dim : dim + 1, :] for offset in range(ORDER)]

        dense_x_ref[index, 1] = dense(base_x, rows(0), 8)
        dense_y_ref[index, 1] = dense(base_y, rows(1), PATCH_Y)
        high, low = split(dense(rest, rows(2), FAN))
        joined = jnp.concatenate([high, low, high], axis=0)
        parts = dot(table_z_ref[2 * CZ : 4 * CZ, : 3 * FAN], joined)
        wave = turn_ref[index, :CZ] * parts[:CZ] + turn_ref[index, CZ:] * parts[CZ:]
        high, low = split(wave)
        z_ref[index, 2 * CZ : 3 * CZ] = high
        z_ref[index, 3 * CZ :] = low

    def spread(index, part):
        plain_y = dense_y_ref[index, 0]
        patch = jnp.concatenate(
            [dense_x_ref[index, 2, x : x + 1, :] * plain_y for x in range(CX)], axis=0
        )
        high, low = split(patch)
        both = dot(high, z_ref[index, 0 : 2 * CZ], True)
        summed = both[:, :CZ] + both[:, CZ:] + dot(low, z_ref[index, 0:CZ], True)
        rows = pl.ds(pl.multiple_of(part * CY, CY), PATCH_Y)
        for x in range(CX):
            acc_ref[x, rows, :] += summed[x * PATCH_Y : (x + 1) * PATCH_Y]

    near = [(0, sibling), (1, col), (1, sibling)]
    far = [(behind, other) for other in far_cols for behind in range(2)]
    fetches[0].wait()
    prepare(col, 0)
    pl.semaphore_wait(barrier, ROWS - 1 + 3 * (COLS - 1))

    for group, members in enumerate((far, near)):
        for behind, other in members:
            remote(
                atoms_ref.at[col],
                atoms_ref.at[behind * COLS + col],
                send_sems.at[0],
                atoms_sems.at[group],
                row_after if behind else row,
                other,
            ).start()
    spread(col, col)
    for group, members in ((1, near), (0, far)):
        count = len(members)
        remote(
            atoms_ref.at[0:count],
            atoms_ref.at[0:count],
            send_sems.at[0],
            atoms_sems.at[group],
            row_after,
            col,
        ).wait_recv()
        for behind, other in members:
            prepare(behind * COLS + other, behind)
        for behind, other in members:
            spread(behind * COLS + other, other)

    fetches[1].wait()
    for x in range(CX):
        acc_ref[x, 0:8, :] += acc_ref[x, KY : KY + 8, :]
    send_flat = send_ref.reshape(HALVES, CX, KY // HALVES, CZ)
    field = jnp.concatenate([acc_ref[x, :KY] for x in range(CX)], axis=1)
    high, low = split(field)
    for half in range(HALVES):
        rows = slice(half * KY // HALVES, (half + 1) * KY // HALVES)
        result = dot3(table_y_ref[0, rows], table_y_ref[1, rows], high, low)
        for x in range(CX):
            send_flat[half, x] = result[:, x * CZ : (x + 1) * CZ]

        @pl.loop(1, ROWS)
        def _(step):
            target = lax.rem(row + step, ROWS)
            remote(
                send_ref.at[half, :, target],
                turned_ref.at[half, row],
                send_sems.at[1],
                turned_sems.at[half],
                target,
                col,
            ).start()

        turned_ref[half, row] = send_ref[half, :, row]

    for behind in range(2):
        for part in far_cols + [col, sibling]:
            prepare_slopes(behind * COLS + part, behind)
    fetches[2].wait()
    fetches[3].wait()
    count = CX // GATHER_GROUPS
    back_flat = back_ref.reshape(HALVES, KX * PART, CZ)
    turned_flat = turned_ref.reshape(HALVES, KX * PART, CZ)
    for half in range(HALVES):
        influence = jnp.concatenate(
            [
                influence_ref[pl.ds(half * PART + j, KX, stride=WIDTH), :]
                for j in range(PART)
            ],
            axis=1,
        )
        remote(
            turned_ref.at[half, 0 : ROWS - 1],
            turned_ref.at[half, 0 : ROWS - 1],
            send_sems.at[1],
            turned_sems.at[half],
            row_after,
            col,
        ).wait_recv()
        field = jnp.concatenate(
            [turned_flat[half, pl.ds(j, KX, stride=PART), :] for j in range(PART)], axis=1
        )
        high, low = split(field)
        spectrum = influence * dot3(table_x_ref[0, :KX], table_x_ref[1, :KX], high, low)
        high, low = split(spectrum)
        result = dot3(table_x_ref[0, :KX], table_x_ref[1, :KX], high, low)
        for j in range(PART):
            back_flat[half, pl.ds(j, KX, stride=PART), :] = result[:, j * CZ : (j + 1) * CZ]
        pieces = 1 if half < HALVES - 1 else GATHER_GROUPS
        for piece in range(pieces):
            planes = pl.ds(piece * (CX // pieces), CX // pieces)

            @pl.loop(1, ROWS)
            def _(step):
                target = lax.rem(row + step, ROWS)
                remote(
                    back_ref.at[half, target, planes],
                    returned_ref.at[half, planes, row],
                    send_sems.at[2],
                    returned_sems.at[half + piece],
                    target,
                    col,
                ).start()

        returned_ref[half, :, row] = back_ref[half, row]

    def returned(half, planes, place):
        return remote(
            returned_ref.at[half, planes, 0 : ROWS - 1],
            returned_ref.at[half, planes, 0 : ROWS - 1],
            send_sems.at[2],
            returned_sems.at[place],
            row_after,
            col,
        )

    fetches[4].wait()
    for half in range(HALVES - 1):
        returned(half, slice(0, CX), half).wait_recv()
    returned_flat = returned_ref.reshape(HALVES, CX, KY // HALVES, CZ)
    order = far + [(1, sibling), (0, sibling), (1, col), (0, col)]
    for group in range(GATHER_GROUPS):
        planes = slice(group * count, (group + 1) * count)
        returned(HALVES - 1, planes, HALVES - 1 + group).wait_recv()
        field = jnp.concatenate(
            [
                jnp.concatenate(
                    [returned_flat[half, group * count + x] for half in range(HALVES)], axis=0
                )
                for x in range(count)
            ],
            axis=1,
        )
        high, low = split(field)
        result = dot3(table_back_ref[0], table_back_ref[1], high, low)
        for x in range(count):
            acc_ref[x] = result[:, x * CZ : (x + 1) * CZ]
        for behind, part in order:
            index = behind * COLS + part
            plain_y = dense_y_ref[index, 0]
            slope_y = dense_y_ref[index, 1]
            rows = pl.ds(pl.multiple_of(part * CY, CY), PATCH_Y)
            patch = jnp.concatenate([acc_ref[x, rows, :] for x in range(count)], axis=0)
            high, low = split(patch)
            both = jnp.concatenate([high, low], axis=1)

            def contract(place):
                wave_high = z_ref[index, place * CZ : (place + 1) * CZ]
                wave_low = z_ref[index, (place + 1) * CZ : (place + 2) * CZ]
                twice = jnp.concatenate([wave_high, wave_high], axis=0)
                return dot(both, twice) + dot(high, wave_low)

            plain = contract(0)
            third = contract(2)
            if group == 0:
                sums = [0.0] * 4
            else:
                sums = [partial_ref[index, k : k + 1] for k in range(4)]
            for x in range(count):
                here = plain[x * PATCH_Y : (x + 1) * PATCH_Y]
                there = third[x * PATCH_Y : (x + 1) * PATCH_Y]
                inner = jnp.sum(plain_y * here, axis=0, keepdims=True)
                along_y = jnp.sum(slope_y * here, axis=0, keepdims=True)
                along_z = jnp.sum(plain_y * there, axis=0, keepdims=True)
                place = group * count + x
                plain_x = dense_x_ref[index, 0, place : place + 1, :]
                slope_x = dense_x_ref[index, 1, place : place + 1, :]
                sums[0] = sums[0] + plain_x * inner
                sums[1] = sums[1] + slope_x * inner
                sums[2] = sums[2] + plain_x * along_y
                sums[3] = sums[3] + plain_x * along_z
            for k in range(4):
                partial_ref[index, k : k + 1] = sums[k]
            if group == GATHER_GROUPS - 1 and not (behind == 0 and part is col):
                remote(
                    partial_ref.at[index],
                    arrived_ref.at[behind * COLS + col],
                    send_sems.at[3],
                    arrived_sem,
                    row_before if behind else row,
                    part,
                ).start()

    arrived_ref[col] = partial_ref[col]
    remote(
        arrived_ref.at[0 : BLOCKS - 1],
        arrived_ref.at[0 : BLOCKS - 1],
        send_sems.at[3],
        arrived_sem,
        row_after,
        col,
    ).wait()
    total = arrived_ref[0]
    for index in range(1, BLOCKS):
        total = total + arrived_ref[index]
    out_ref[...] = total
    remote(
        atoms_ref.at[0 : BLOCKS - 1],
        atoms_ref.at[0 : BLOCKS - 1],
        send_sems.at[0],
        atoms_sems.at[0],
        row_after,
        col,
    ).wait_send()
    remote(
        turned_ref.at[:, 0 : ROWS - 1],
        turned_ref.at[:, 0 : ROWS - 1],
        send_sems.at[1],
        turned_sems.at[0],
        row_after,
        col,
    ).wait_send()
    returned(slice(0, HALVES), slice(0, CX), 0).wait_send()


def finish_kernel(total_ref, charges_ref, counts_ref, out_charges_ref, out_coords_ref):
    slot = lax.broadcasted_iota(jnp.int32, (1, SLOTS), 1)
    live = slot < counts_ref[0]
    out_charges_ref[...] = jnp.where(live, total_ref[0:1], 0.0)
    out_coords_ref[...] = jnp.where(live, charges_ref[...], 0.0) * total_ref[1:4]


def shape(dims, kind=FLOAT):
    return jax.ShapeDtypeStruct(dims, kind)


def per_device(charges, fractions, base_cells, counts, influence):
    tables = [jnp.asarray(t) for t in make_tables()]
    anywhere = pl.BlockSpec(memory_space=pltpu.HBM)
    vector = pl.BlockSpec(memory_space=pltpu.VMEM)
    scalar = pl.BlockSpec(memory_space=pltpu.SMEM)
    dma = pltpu.SemaphoreType.DMA
    charges = charges.reshape(1, SLOTS)
    total = pl.pallas_call(
        kernel,
        out_shape=shape((4, SLOTS)),
        in_specs=[vector, vector, vector, scalar] + [anywhere] * 5,
        out_specs=vector,
        scratch_shapes=[
            pltpu.VMEM((KX * WIDTH, CZ), FLOAT),
            pltpu.VMEM(tables[0].shape, HIGH_TYPE),
            pltpu.VMEM(tables[1].shape, HIGH_TYPE),
            pltpu.VMEM(tables[2].shape, HIGH_TYPE),
            pltpu.VMEM(tables[3].shape[1:], HIGH_TYPE),
            pltpu.VMEM((BLOCKS, 8, SLOTS), FLOAT),
            pltpu.VMEM((BLOCKS, ORDER, 8, SLOTS), FLOAT),
            pltpu.VMEM((BLOCKS, 3, 8, SLOTS), FLOAT),
            pltpu.VMEM((BLOCKS, 2, PATCH_Y, SLOTS), FLOAT),
            pltpu.VMEM((BLOCKS, 4 * CZ, SLOTS), HIGH_TYPE),
            pltpu.VMEM((BLOCKS, 2 * CZ, SLOTS), FLOAT),
            pltpu.VMEM((CX, KY + 8, CZ), FLOAT),
            pltpu.VMEM((HALVES, CX, ROWS, PART, CZ), FLOAT),
            pltpu.VMEM((HALVES, ROWS, CX, PART, CZ), FLOAT),
            pltpu.VMEM((HALVES, ROWS, CX, PART, CZ), FLOAT),
            pltpu.VMEM((HALVES, CX, ROWS, PART, CZ), FLOAT),
            pltpu.VMEM((BLOCKS, 4, SLOTS), FLOAT),
            pltpu.VMEM((BLOCKS, 4, SLOTS), FLOAT),
            dma((5,)),
            dma((4,)),
            dma((2,)),
            dma((HALVES,)),
            dma((HALVES - 1 + GATHER_GROUPS,)),
            dma,
        ],
        compiler_params=pltpu.CompilerParams(
            collective_id=0, has_side_effects=True, vmem_limit_bytes=VMEM_LIMIT
        ),
    )(charges, fractions, base_cells, counts, influence.reshape(KX * WIDTH, CZ), *tables)
    grad_charges, grad_coords = pl.pallas_call(
        finish_kernel,
        out_shape=(shape((1, SLOTS)), shape((3, SLOTS))),
        in_specs=[vector, vector, scalar],
        out_specs=(vector, vector),
        compiler_params=pltpu.CompilerParams(vmem_limit_bytes=VMEM_LIMIT),
    )(total, charges, counts)
    return grad_charges.reshape(SLOTS), grad_coords


def solution(mesh):
    return jax.shard_map(
        per_device,
        mesh=mesh,
        in_specs=(
            P(("row", "col")),
            P(None, ("row", "col")),
            P(None, ("row", "col")),
            P(("row", "col")),
            P(None, "row", "col"),
        ),
        out_specs=(P(("row", "col")), P(None, ("row", "col"))),
        check_vma=False,
    )
```

time: 75.6 us -> 70 us (0.926)
  the two profiles are of different devices: /device:TPU:1 before, /device:TPU:121 now
where the time goes in v4:
time: 70 us; the launch traced here: 69.7 us
  Pallas kernels  68.4 us (98%)
  between operations  1.29 us (2%)
    pallas_call x1, Pallas kernels, per_device(): pl.pallas_call(kernel, out_shape=shape((4, SLOTS)), in_specs=[vector, vec...  67.1 us

profile of v4, /device:TPU:121, one launch (start us, length us, event | category | flops | bytes accessed | tf_op | source)
XLA Modules:
  0.0 69.7 jit_solution(7662736658659016973)
XLA Ops:
  1.3 67.1 %shard_map.104.total_ref = f32[4,512]{1,0:T(4,128)} custom-call(f32[1,512]{1,0:T(1,128)} %bitcast.4, f32[3,512]{1,0:T(4,128)} %fractions_ref.1, s32[3,512]{1,0:T(4,128)} %cells_ref.1, s32[1]{0:T(128)S(6)} %copy.11.counts_ref, f32[1536,128]{1,0:T(8,128)} %bitcast.3, bf16[2,392,384]{2,1,0:T(8,128)(2,1)} %constant.8.clone.table_x_hbm, ...), custom_call_target="tpu_custom_call" | custom-call | tf_op jit(solution)/shard_map/pallas_call | solution.py:514
  68.4 1.3 %shard_map.105 = (f32[1,512]{1,0:T(1,128)}, f32[3,512]{1,0:T(4,128)}) custom-call(f32[4,512]{1,0:T(4,128)} %shard_map.104.total_ref, f32[1,512]{1,0:T(1,128)} %bitcast.5, s32[1]{0:T(128)S(6)} %copy.11.counts_ref), custom_call_target="tpu_custom_call" | custom-call | tf_op jit(solution)/shard_map/pallas_call | solution.py:549

commit v5 on v4

--- a/solution.py
+++ b/solution.py
@@ -24,11 +24,12 @@
 COARSE = KZ // FINE
 FAN = 2 * FINE
 VMEM_LIMIT = 63 * 1024 * 1024
-GATHER_GROUPS = 1
 HALVES = 2
 WIDTH = KY // ROWS
 PART = WIDTH // HALVES
-BLOCKS = 2 * COLS
+SIDES = 2
+SIDE = ROWS // SIDES
+BLOCKS = 2 * SIDES * COLS
 MESH = pl.DeviceIdType.MESH
 
 HIGH_TYPE = jnp.bfloat16
@@ -50,11 +51,12 @@
     kx = np.arange(KX)
     table_x = np.zeros((2, KX + 8, KX), ml_dtypes.bfloat16)
     table_x[:, :KX] = split_table(cas(kx[:, None] * kx[None, :], KX))
-    ky = np.arange(KY).reshape(ROWS, HALVES, PART).transpose(1, 0, 2).reshape(KY)
+    ky = np.arange(KY).reshape(SIDES, SIDE, HALVES, PART).transpose(0, 2, 1, 3)
+    ky = ky.reshape(SIDES, KY // SIDES)
     y = np.arange(KY + 8)
-    table_y = np.stack(split_table(cas(ky[:, None] * np.arange(KY)[None, :], KY)))
-    table_y = np.pad(table_y, ((0, 0), (0, 8), (0, 0)))
-    table_back = np.stack(split_table(cas(y[:, None] * ky[None, :], KY)))
+    table_y = np.stack(split_table(cas(ky[:, :, None] * np.arange(KY), KY)), axis=1)
+    table_y = np.pad(table_y, ((0, 0), (0, 0), (0, 8), (0, 0)))
+    table_back = np.stack(split_table(cas(y[None, :, None] * ky[:, None, :], KY)), axis=1)
     kz = np.arange(KZ)
     coarse = (kz[:, None] * np.arange(COARSE)[None, :] * FINE % KZ) * (2.0 * math.pi / KZ)
     fine = kz[:, None] * np.arange(FAN)[None, :]
@@ -163,8 +165,14 @@
     col = lax.axis_index("col")
     half_at = col // 2
     core = lax.rem(col, 2)
+    side = row // SIDE
+    place = lax.rem(row, SIDE)
     row_after = lax.rem(row + 1, ROWS)
     row_before = lax.rem(row + ROWS - 1, ROWS)
+
+    def across(device_row):
+        return lax.rem(device_row + SIDE, ROWS)
+
     sibling = half_at * 2 + 1 - core
     far_cols = [(1 - half_at) * 2 + core, (1 - half_at) * 2 + 1 - core]
 
@@ -175,34 +183,39 @@
             barrier, inc=1, device_id=(device_row, device_col), device_id_type=MESH
         )
 
+    others = [across(row)]
+    for device_row in (row_after, row_before):
+        others += [device_row, across(device_row)]
     for other in far_cols + [sibling]:
         greet(row, other)
-        greet(row_after, other)
-        greet(row_before, other)
-
-    @pl.loop(1, ROWS)
+    for other in far_cols + [sibling, col]:
+        for device_row in others:
+            greet(device_row, other)
+
+    @pl.loop(1, SIDE)
     def _(step):
-        greet(lax.rem(row + step, ROWS), col)
+        greet(side * SIDE + lax.rem(place + step, SIDE), col)
 
     fetches = [
         pltpu.make_async_copy(table_z_hbm.at[col], table_z_ref, local_sems.at[0]),
-        pltpu.make_async_copy(table_y_hbm, table_y_ref, local_sems.at[1]),
+        pltpu.make_async_copy(table_y_hbm.at[side], table_y_ref, local_sems.at[1]),
         pltpu.make_async_copy(table_x_hbm, table_x_ref, local_sems.at[2]),
         pltpu.make_async_copy(influence_hbm, influence_ref, local_sems.at[3]),
-        pltpu.make_async_copy(table_back_hbm, table_back_ref, local_sems.at[4]),
+        pltpu.make_async_copy(table_back_hbm.at[side], table_back_ref, local_sems.at[4]),
     ]
     for fetch in fetches:
         fetch.start()
 
     slot = lax.broadcasted_iota(jnp.int32, (1, SLOTS), 1)
+    own = side * 2 * COLS + col
     weight = jnp.where(slot < counts_ref[0], charges_ref[...], 0.0)
-    atoms_ref[col, 0:1, :] = weight
-    atoms_ref[col, 1:4, :] = fractions_ref[...]
+    atoms_ref[own, 0:1, :] = weight
+    atoms_ref[own, 1:4, :] = fractions_ref[...]
     cells = cells_ref[...]
-    atoms_ref[col, 4:5, :] = (cells[0:1] - row * CX).astype(FLOAT)
-    atoms_ref[col, 5:6, :] = (cells[1:2] - col * CY).astype(FLOAT)
-    atoms_ref[col, 6:7, :] = cells[2:3].astype(FLOAT)
-    atoms_ref[col, 7:8, :] = weight
+    atoms_ref[own, 4:5, :] = (cells[0:1] - row * CX).astype(FLOAT)
+    atoms_ref[own, 5:6, :] = (cells[1:2] - col * CY).astype(FLOAT)
+    atoms_ref[own, 6:7, :] = cells[2:3].astype(FLOAT)
+    atoms_ref[own, 7:8, :] = weight
     acc_ref[...] = jnp.zeros(acc_ref.shape, FLOAT)
 
     def remote(source, target, send_sem, recv_sem, device_row, device_col):
@@ -263,7 +276,13 @@
         z_ref[index, 2 * CZ : 3 * CZ] = high
         z_ref[index, 3 * CZ :] = low
 
-    def spread(index, part):
+    def block(member):
+        here, behind, part = member
+        return here * 2 * COLS + behind * COLS + part
+
+    def spread(member):
+        index = block(member)
+        here, _, part = member
         plain_y = dense_y_ref[index, 0]
         patch = jnp.concatenate(
             [dense_x_ref[index, 2, x : x + 1, :] * plain_y for x in range(CX)], axis=0
@@ -273,25 +292,34 @@
         summed = both[:, :CZ] + both[:, CZ:] + dot(low, z_ref[index, 0:CZ], True)
         rows = pl.ds(pl.multiple_of(part * CY, CY), PATCH_Y)
         for x in range(CX):
-            acc_ref[x, rows, :] += summed[x * PATCH_Y : (x + 1) * PATCH_Y]
-
-    near = [(0, sibling), (1, col), (1, sibling)]
-    far = [(behind, other) for other in far_cols for behind in range(2)]
+            acc_ref[here * CX + x, rows, :] += summed[x * PATCH_Y : (x + 1) * PATCH_Y]
+
+    away = 1 - side
+    near = [(away, 0, col), (side, 0, sibling), (away, 0, sibling)]
+    near += [(here, 1, part) for here in (side, away) for part in (col, sibling)]
+    far = [
+        (here, behind, part) for here in (side, away) for behind in range(2) for part in far_cols
+    ]
     fetches[0].wait()
-    prepare(col, 0)
-    pl.semaphore_wait(barrier, ROWS - 1 + 3 * (COLS - 1))
-
-    for group, members in enumerate((far, near)):
-        for behind, other in members:
-            remote(
-                atoms_ref.at[col],
-                atoms_ref.at[behind * COLS + col],
-                send_sems.at[0],
-                atoms_sems.at[group],
-                row_after if behind else row,
-                other,
-            ).start()
-    spread(col, col)
+    prepare(own, 0)
+    pl.semaphore_wait(barrier, 3 + 4 * 5 + SIDE - 1)
+
+    for group, parts in ((0, far_cols), (1, [sibling, col])):
+        for other in parts:
+            for behind, device_row in enumerate((row, row_after)):
+                slot_at = (device_row // SIDE) * 2 * COLS + behind * COLS + col
+                for target in (device_row, across(device_row)):
+                    if other is col and target is row:
+                        continue
+                    remote(
+                        atoms_ref.at[own],
+                        atoms_ref.at[slot_at],
+                        send_sems.at[0],
+                        atoms_sems.at[group],
+                        target,
+                        other,
+                    ).start()
+    spread((side, 0, col))
     for group, members in ((1, near), (0, far)):
         count = len(members)
         remote(
@@ -302,43 +330,45 @@
             row_after,
             col,
         ).wait_recv()
-        for behind, other in members:
-            prepare(behind * COLS + other, behind)
-        for behind, other in members:
-            spread(behind * COLS + other, other)
+        for member in members:
+            prepare(block(member), member[1])
+        for member in members:
+            spread(member)
 
     fetches[1].wait()
-    for x in range(CX):
+    for x in range(SIDES * CX):
         acc_ref[x, 0:8, :] += acc_ref[x, KY : KY + 8, :]
-    send_flat = send_ref.reshape(HALVES, CX, KY // HALVES, CZ)
-    field = jnp.concatenate([acc_ref[x, :KY] for x in range(CX)], axis=1)
-    high, low = split(field)
+    depth = SIDE * PART
+    send_flat = send_ref.reshape(HALVES, SIDES, CX, depth, CZ)
+    fields = [
+        split(jnp.concatenate([acc_ref[here * CX + x, :KY] for x in range(CX)], axis=1))
+        for here in range(SIDES)
+    ]
     for half in range(HALVES):
-        rows = slice(half * KY // HALVES, (half + 1) * KY // HALVES)
-        result = dot3(table_y_ref[0, rows], table_y_ref[1, rows], high, low)
-        for x in range(CX):
-            send_flat[half, x] = result[:, x * CZ : (x + 1) * CZ]
-
-        @pl.loop(1, ROWS)
+        rows = slice(half * depth, (half + 1) * depth)
+        for here in range(SIDES):
+            result = dot3(table_y_ref[0, rows], table_y_ref[1, rows], *fields[here])
+            for x in range(CX):
+                send_flat[half, here, x] = result[:, x * CZ : (x + 1) * CZ]
+
+        @pl.loop(1, SIDE)
         def _(step):
-            target = lax.rem(row + step, ROWS)
+            target = lax.rem(place + step, SIDE)
             remote(
-                send_ref.at[half, :, target],
-                turned_ref.at[half, row],
+                send_ref.at[half, :, :, target],
+                turned_ref.at[half, :, place],
                 send_sems.at[1],
                 turned_sems.at[half],
-                target,
+                side * SIDE + target,
                 col,
             ).start()
 
-        turned_ref[half, row] = send_ref[half, :, row]
-
-    for behind in range(2):
-        for part in far_cols + [col, sibling]:
-            prepare_slopes(behind * COLS + part, behind)
+        turned_ref[half, :, place] = send_ref[half, :, :, place]
+
+    for member in far + near + [(side, 0, col)]:
+        prepare_slopes(block(member), member[1])
     fetches[2].wait()
     fetches[3].wait()
-    count = CX // GATHER_GROUPS
     back_flat = back_ref.reshape(HALVES, KX * PART, CZ)
     turned_flat = turned_ref.reshape(HALVES, KX * PART, CZ)
     for half in range(HALVES):
@@ -350,8 +380,8 @@
             axis=1,
         )
         remote(
-            turned_ref.at[half, 0 : ROWS - 1],
-            turned_ref.at[half, 0 : ROWS - 1],
+            turned_ref.at[half, :, 0 : SIDE - 1],
+            turned_ref.at[half, :, 0 : SIDE - 1],
             send_sems.at[1],
             turned_sems.at[half],
             row_after,
@@ -366,102 +396,89 @@
         result = dot3(table_x_ref[0, :KX], table_x_ref[1, :KX], high, low)
         for j in range(PART):
             back_flat[half, pl.ds(j, KX, stride=PART), :] = result[:, j * CZ : (j + 1) * CZ]
-        pieces = 1 if half < HALVES - 1 else GATHER_GROUPS
-        for piece in range(pieces):
-            planes = pl.ds(piece * (CX // pieces), CX // pieces)
-
-            @pl.loop(1, ROWS)
-            def _(step):
-                target = lax.rem(row + step, ROWS)
-                remote(
-                    back_ref.at[half, target, planes],
-                    returned_ref.at[half, planes, row],
-                    send_sems.at[2],
-                    returned_sems.at[half + piece],
-                    target,
-                    col,
-                ).start()
-
-        returned_ref[half, :, row] = back_ref[half, row]
-
-    def returned(half, planes, place):
-        return remote(
-            returned_ref.at[half, planes, 0 : ROWS - 1],
-            returned_ref.at[half, planes, 0 : ROWS - 1],
+
+        @pl.loop(1, SIDE)
+        def _(step):
+            target = lax.rem(place + step, SIDE)
+            remote(
+                back_ref.at[half, :, target],
+                returned_ref.at[half, :, :, place],
+                send_sems.at[2],
+                returned_sems.at[half],
+                side * SIDE + target,
+                col,
+            ).start()
+
+        returned_ref[half, :, :, place] = back_ref[half, :, place]
+
+    fetches[4].wait()
+    for half in range(HALVES):
+        remote(
+            returned_ref.at[half, :, :, 0 : SIDE - 1],
+            returned_ref.at[half, :, :, 0 : SIDE - 1],
             send_sems.at[2],
-            returned_sems.at[place],
+            returned_sems.at[half],
             row_after,
             col,
-        )
-
-    fetches[4].wait()
-    for half in range(HALVES - 1):
-        returned(half, slice(0, CX), half).wait_recv()
-    returned_flat = returned_ref.reshape(HALVES, CX, KY // HALVES, CZ)
-    order = far + [(1, sibling), (0, sibling), (1, col), (0, col)]
-    for group in range(GATHER_GROUPS):
-        planes = slice(group * count, (group + 1) * count)
-        returned(HALVES - 1, planes, HALVES - 1 + group).wait_recv()
+        ).wait_recv()
+    returned_flat = returned_ref.reshape(HALVES, SIDES, CX, depth, CZ)
+    for here in range(SIDES):
         field = jnp.concatenate(
             [
-                jnp.concatenate(
-                    [returned_flat[half, group * count + x] for half in range(HALVES)], axis=0
-                )
-                for x in range(count)
+                jnp.concatenate([returned_flat[half, here, x] for half in range(HALVES)], axis=0)
+                for x in range(CX)
             ],
             axis=1,
         )
         high, low = split(field)
         result = dot3(table_back_ref[0], table_back_ref[1], high, low)
-        for x in range(count):
-            acc_ref[x] = result[:, x * CZ : (x + 1) * CZ]
-        for behind, part in order:
-            index = behind * COLS + part
-            plain_y = dense_y_ref[index, 0]
-            slope_y = dense_y_ref[index, 1]
-            rows = pl.ds(pl.multiple_of(part * CY, CY), PATCH_Y)
-            patch = jnp.concatenate([acc_ref[x, rows, :] for x in range(count)], axis=0)
-            high, low = split(patch)
-            both = jnp.concatenate([high, low], axis=1)
-
-            def contract(place):
-                wave_high = z_ref[index, place * CZ : (place + 1) * CZ]
-                wave_low = z_ref[index, (place + 1) * CZ : (place + 2) * CZ]
-                twice = jnp.concatenate([wave_high, wave_high], axis=0)
-                return dot(both, twice) + dot(high, wave_low)
-
-            plain = contract(0)
-            third = contract(2)
-            if group == 0:
-                sums = [0.0] * 4
-            else:
-                sums = [partial_ref[index, k : k + 1] for k in range(4)]
-            for x in range(count):
-                here = plain[x * PATCH_Y : (x + 1) * PATCH_Y]
-                there = third[x * PATCH_Y : (x + 1) * PATCH_Y]
-                inner = jnp.sum(plain_y * here, axis=0, keepdims=True)
-                along_y = jnp.sum(slope_y * here, axis=0, keepdims=True)
-                along_z = jnp.sum(plain_y * there, axis=0, keepdims=True)
-                place = group * count + x
-                plain_x = dense_x_ref[index, 0, place : place + 1, :]
-                slope_x = dense_x_ref[index, 1, place : place + 1, :]
-                sums[0] = sums[0] + plain_x * inner
-                sums[1] = sums[1] + slope_x * inner
-                sums[2] = sums[2] + plain_x * along_y
-                sums[3] = sums[3] + plain_x * along_z
-            for k in range(4):
-                partial_ref[index, k : k + 1] = sums[k]
-            if group == GATHER_GROUPS - 1 and not (behind == 0 and part is col):
-                remote(
-                    partial_ref.at[index],
-                    arrived_ref.at[behind * COLS + col],
-                    send_sems.at[3],
-                    arrived_sem,
-                    row_before if behind else row,
-                    part,
-                ).start()
-
-    arrived_ref[col] = partial_ref[col]
+        for x in range(CX):
+            acc_ref[here * CX + x] = result[:, x * CZ : (x + 1) * CZ]
+    mine = (side, 0, col)
+    for member in far + near + [mine]:
+        here, behind, part = member
+        index = block(member)
+        plain_y = dense_y_ref[index, 0]
+        slope_y = dense_y_ref[index, 1]
+        rows = pl.ds(pl.multiple_of(part * CY, CY), PATCH_Y)
+        patch = jnp.concatenate([acc_ref[here * CX + x, rows, :] for x in range(CX)], axis=0)
+        high, low = split(patch)
+        both = jnp.concatenate([high, low], axis=1)
+
+        def contract(place_at):
+            wave_high = z_ref[index, place_at * CZ : (place_at + 1) * CZ]
+            wave_low = z_ref[index, (place_at + 1) * CZ : (place_at + 2) * CZ]
+            twice = jnp.concatenate([wave_high, wave_high], axis=0)
+            return dot(both, twice) + dot(high, wave_low)
+
+        plain = contract(0)
+        third = contract(2)
+        sums = [0.0] * 4
+        for x in range(CX):
+            first_part = plain[x * PATCH_Y : (x + 1) * PATCH_Y]
+            third_part = third[x * PATCH_Y : (x + 1) * PATCH_Y]
+            inner = jnp.sum(plain_y * first_part, axis=0, keepdims=True)
+            along_y = jnp.sum(slope_y * first_part, axis=0, keepdims=True)
+            along_z = jnp.sum(plain_y * third_part, axis=0, keepdims=True)
+            plain_x = dense_x_ref[index, 0, x : x + 1, :]
+            slope_x = dense_x_ref[index, 1, x : x + 1, :]
+            sums[0] = sums[0] + plain_x * inner
+            sums[1] = sums[1] + slope_x * inner
+            sums[2] = sums[2] + plain_x * along_y
+            sums[3] = sums[3] + plain_x * along_z
+        for k in range(4):
+            partial_ref[index, k : k + 1] = sums[k]
+        if member is not mine:
+            remote(
+                partial_ref.at[index],
+                arrived_ref.at[behind * SIDES * COLS + side * COLS + col],
+                send_sems.at[3],
+                arrived_sem,
+                lax.rem(here * SIDE + place + ROWS - behind, ROWS),
+                part,
+            ).start()
+
+    arrived_ref[side * COLS + col] = partial_ref[own]
     remote(
         arrived_ref.at[0 : BLOCKS - 1],
         arrived_ref.at[0 : BLOCKS - 1],
@@ -483,14 +500,21 @@
         col,
     ).wait_send()
     remote(
-        turned_ref.at[:, 0 : ROWS - 1],
-        turned_ref.at[:, 0 : ROWS - 1],
+        turned_ref.at[:, :, 0 : SIDE - 1],
+        turned_ref.at[:, :, 0 : SIDE - 1],
         send_sems.at[1],
         turned_sems.at[0],
         row_after,
         col,
     ).wait_send()
-    returned(slice(0, HALVES), slice(0, CX), 0).wait_send()
+    remote(
+        returned_ref.at[:, :, :, 0 : SIDE - 1],
+        returned_ref.at[:, :, :, 0 : SIDE - 1],
+        send_sems.at[2],
+        returned_sems.at[0],
+        row_after,
+        col,
+    ).wait_send()
 
 
 def finish_kernel(total_ref, charges_ref, counts_ref, out_charges_ref, out_coords_ref):
@@ -519,8 +543,8 @@
         scratch_shapes=[
             pltpu.VMEM((KX * WIDTH, CZ), FLOAT),
             pltpu.VMEM(tables[0].shape, HIGH_TYPE),
-            pltpu.VMEM(tables[1].shape, HIGH_TYPE),
-            pltpu.VMEM(tables[2].shape, HIGH_TYPE),
+            pltpu.VMEM(tables[1].shape[1:], HIGH_TYPE),
+            pltpu.VMEM(tables[2].shape[1:], HIGH_TYPE),
             pltpu.VMEM(tables[3].shape[1:], HIGH_TYPE),
             pltpu.VMEM((BLOCKS, 8, SLOTS), FLOAT),
             pltpu.VMEM((BLOCKS, ORDER, 8, SLOTS), FLOAT),
@@ -528,18 +552,18 @@
             pltpu.VMEM((BLOCKS, 2, PATCH_Y, SLOTS), FLOAT),
             pltpu.VMEM((BLOCKS, 4 * CZ, SLOTS), HIGH_TYPE),
             pltpu.VMEM((BLOCKS, 2 * CZ, SLOTS), FLOAT),
-            pltpu.VMEM((CX, KY + 8, CZ), FLOAT),
-            pltpu.VMEM((HALVES, CX, ROWS, PART, CZ), FLOAT),
-            pltpu.VMEM((HALVES, ROWS, CX, PART, CZ), FLOAT),
-            pltpu.VMEM((HALVES, ROWS, CX, PART, CZ), FLOAT),
-            pltpu.VMEM((HALVES, CX, ROWS, PART, CZ), FLOAT),
+            pltpu.VMEM((SIDES * CX, KY + 8, CZ), FLOAT),
+            pltpu.VMEM((HALVES, SIDES, CX, SIDE, PART, CZ), FLOAT),
+            pltpu.VMEM((HALVES, SIDES, SIDE, CX, PART, CZ), FLOAT),
+            pltpu.VMEM((HALVES, SIDES, SIDE, CX, PART, CZ), FLOAT),
+            pltpu.VMEM((HALVES, SIDES, CX, SIDE, PART, CZ), FLOAT),
             pltpu.VMEM((BLOCKS, 4, SLOTS), FLOAT),
             pltpu.VMEM((BLOCKS, 4, SLOTS), FLOAT),
             dma((5,)),
             dma((4,)),
             dma((2,)),
             dma((HALVES,)),
-            dma((HALVES - 1 + GATHER_GROUPS,)),
+            dma((HALVES,)),
             dma,
         ],
         compiler_params=pltpu.CompilerParams(

time: 70 us -> 70.5 us (level)
  the two profiles are of different devices: /device:TPU:121 before, /device:TPU:1 now
where the time goes in v5:
time: 70.5 us; the launch traced here: 70.2 us
  Pallas kernels  68.9 us (98%)
  between operations  1.29 us (2%)
    pallas_call x1, Pallas kernels, per_device(): pl.pallas_call(kernel, out_shape=shape((4, SLOTS)), in_specs=[vector, vec...  67.6 us

profile of v5, /device:TPU:1, one launch (start us, length us, event | category | flops | bytes accessed | tf_op | source)
XLA Modules:
  0.0 70.2 jit_solution(3228124772880888097)
XLA Ops:
  1.3 67.6 %shard_map.104.total_ref = f32[4,512]{1,0:T(4,128)} custom-call(f32[1,512]{1,0:T(1,128)} %bitcast.4, f32[3,512]{1,0:T(4,128)} %fractions_ref.1, s32[3,512]{1,0:T(4,128)} %cells_ref.1, s32[1]{0:T(128)S(6)} %copy.11.counts_ref, f32[1536,128]{1,0:T(8,128)} %bitcast.3, bf16[2,392,384]{2,1,0:T(8,128)(2,1)} %constant.8.clone.table_x_hbm, ...), custom_call_target="tpu_custom_call" | custom-call | tf_op jit(solution)/shard_map/pallas_call | solution.py:538
  68.9 1.3 %shard_map.105 = (f32[1,512]{1,0:T(1,128)}, f32[3,512]{1,0:T(4,128)}) custom-call(f32[4,512]{1,0:T(4,128)} %shard_map.104.total_ref, f32[1,512]{1,0:T(1,128)} %bitcast.5, s32[1]{0:T(128)S(6)} %copy.11.counts_ref), custom_call_target="tpu_custom_call" | custom-call | tf_op jit(solution)/shard_map/pallas_call | solution.py:573

commit v6 on v5

--- a/solution.py
+++ b/solution.py
@@ -320,8 +320,10 @@
                         other,
                     ).start()
     spread((side, 0, col))
-    for group, members in ((1, near), (0, far)):
-        count = len(members)
+    depth = SIDE * PART
+    send_flat = send_ref.reshape(HALVES, SIDES, CX, depth, CZ)
+
+    def arrive(group, count):
         remote(
             atoms_ref.at[0:count],
             atoms_ref.at[0:count],
@@ -330,39 +332,42 @@
             row_after,
             col,
         ).wait_recv()
+
+    def work(members):
         for member in members:
             prepare(block(member), member[1])
         for member in members:
             spread(member)
 
-    fetches[1].wait()
-    for x in range(SIDES * CX):
-        acc_ref[x, 0:8, :] += acc_ref[x, KY : KY + 8, :]
-    depth = SIDE * PART
-    send_flat = send_ref.reshape(HALVES, SIDES, CX, depth, CZ)
-    fields = [
-        split(jnp.concatenate([acc_ref[here * CX + x, :KY] for x in range(CX)], axis=1))
-        for here in range(SIDES)
-    ]
-    for half in range(HALVES):
-        rows = slice(half * depth, (half + 1) * depth)
-        for here in range(SIDES):
-            result = dot3(table_y_ref[0, rows], table_y_ref[1, rows], *fields[here])
+    arrive(1, len(near))
+    work(near)
+    arrive(0, len(far))
+    for here in (away, side):
+        work([member for member in far if member[0] is here])
+        if here is away:
+            fetches[1].wait()
+        for x in range(CX):
+            acc_ref[here * CX + x, 0:8, :] += acc_ref[here * CX + x, KY : KY + 8, :]
+        field = split(jnp.concatenate([acc_ref[here * CX + x, :KY] for x in range(CX)], axis=1))
+        for half in range(HALVES):
+            rows = slice(half * depth, (half + 1) * depth)
+            result = dot3(table_y_ref[0, rows], table_y_ref[1, rows], *field)
             for x in range(CX):
                 send_flat[half, here, x] = result[:, x * CZ : (x + 1) * CZ]
 
-        @pl.loop(1, SIDE)
-        def _(step):
-            target = lax.rem(place + step, SIDE)
-            remote(
-                send_ref.at[half, :, :, target],
-                turned_ref.at[half, :, place],
-                send_sems.at[1],
-                turned_sems.at[half],
-                side * SIDE + target,
-                col,
-            ).start()
-
+            @pl.loop(1, SIDE)
+            def _(step):
+                target = lax.rem(place + step, SIDE)
+                remote(
+                    send_ref.at[half, here, :, target],
+                    turned_ref.at[half, here, place],
+                    send_sems.at[1],
+                    turned_sems.at[half],
+                    side * SIDE + target,
+                    col,
+                ).start()
+
+    for half in range(HALVES):
         turned_ref[half, :, place] = send_ref[half, :, :, place]
 
     for member in far + near + [(side, 0, col)]:
@@ -397,32 +402,46 @@
         for j in range(PART):
             back_flat[half, pl.ds(j, KX, stride=PART), :] = result[:, j * CZ : (j + 1) * CZ]
 
-        @pl.loop(1, SIDE)
-        def _(step):
-            target = lax.rem(place + step, SIDE)
-            remote(
-                back_ref.at[half, :, target],
-                returned_ref.at[half, :, :, place],
-                send_sems.at[2],
-                returned_sems.at[half],
-                side * SIDE + target,
-                col,
-            ).start()
+        if half < HALVES - 1:
+            pieces = [slice(0, SIDES)]
+        else:
+            pieces = [away, side]
+        for number, here in enumerate(pieces):
+
+            @pl.loop(1, SIDE)
+            def _(step):
+                target = lax.rem(place + step, SIDE)
+                source = back_ref.at[half, here, target]
+                landing = returned_ref.at[half, here, :, place]
+                remote(
+                    source,
+                    landing,
+                    send_sems.at[2],
+                    returned_sems.at[half + number],
+                    side * SIDE + target,
+                    col,
+                ).start()
 
         returned_ref[half, :, :, place] = back_ref[half, :, place]
 
     fetches[4].wait()
-    for half in range(HALVES):
+    def returned(half, here, number):
         remote(
-            returned_ref.at[half, :, :, 0 : SIDE - 1],
-            returned_ref.at[half, :, :, 0 : SIDE - 1],
+            returned_ref.at[half, here, :, 0 : SIDE - 1],
+            returned_ref.at[half, here, :, 0 : SIDE - 1],
             send_sems.at[2],
-            returned_sems.at[half],
+            returned_sems.at[number],
             row_after,
             col,
         ).wait_recv()
+
+    for half in range(HALVES - 1):
+        returned(half, slice(0, SIDES), half)
     returned_flat = returned_ref.reshape(HALVES, SIDES, CX, depth, CZ)
-    for here in range(SIDES):
+    mine = (side, 0, col)
+
+    def collect(number, here):
+        returned(HALVES - 1, here, HALVES - 1 + number)
         field = jnp.concatenate(
             [
                 jnp.concatenate([returned_flat[half, here, x] for half in range(HALVES)], axis=0)
@@ -434,8 +453,7 @@
         result = dot3(table_back_ref[0], table_back_ref[1], high, low)
         for x in range(CX):
             acc_ref[here * CX + x] = result[:, x * CZ : (x + 1) * CZ]
-    mine = (side, 0, col)
-    for member in far + near + [mine]:
+    def contribute(member):
         here, behind, part = member
         index = block(member)
         plain_y = dense_y_ref[index, 0]
@@ -477,6 +495,14 @@
                 lax.rem(here * SIDE + place + ROWS - behind, ROWS),
                 part,
             ).start()
+
+    for number, here in enumerate((away, side)):
+        collect(number, here)
+        members = [member for member in far + near if member[0] is here]
+        if here is side:
+            members.append(mine)
+        for member in members:
+            contribute(member)
 
     arrived_ref[side * COLS + col] = partial_ref[own]
     remote(
@@ -563,7 +589,7 @@
             dma((4,)),
             dma((2,)),
             dma((HALVES,)),
-            dma((HALVES,)),
+            dma((HALVES + SIDES - 1,)),
             dma,
         ],
         compiler_params=pltpu.CompilerParams(

time: 70.5 us -> 67.6 us (0.959)
  Pallas kernels: 68.9 us -> 66.1 us
    pallas_call x1, Pallas kernels: 67.6 us -> 64.8 us  [per_device(): pl.pallas_call(kernel, out_shape=shape((4, SLOTS)), in_specs=[vector, vec...]
where the time goes in v6:
time: 67.6 us; the launch traced here: 67.4 us
  Pallas kernels  66.1 us (98%)
  between operations  1.29 us (2%)
    pallas_call x1, Pallas kernels, per_device(): pl.pallas_call(kernel, out_shape=shape((4, SLOTS)), in_specs=[vector, vec...  64.8 us

profile of v6, /device:TPU:1, one launch (start us, length us, event | category | flops | bytes accessed | tf_op | source)
XLA Modules:
  0.0 67.4 jit_solution(9394583463721178425)
XLA Ops:
  1.3 64.8 %shard_map.104.total_ref = f32[4,512]{1,0:T(4,128)} custom-call(f32[1,512]{1,0:T(1,128)} %bitcast.4, f32[3,512]{1,0:T(4,128)} %fractions_ref.1, s32[3,512]{1,0:T(4,128)} %cells_ref.1, s32[1]{0:T(128)S(6)} %copy.11.counts_ref, f32[1536,128]{1,0:T(8,128)} %bitcast.3, bf16[2,392,384]{2,1,0:T(8,128)(2,1)} %constant.8.clone.table_x_hbm, ...), custom_call_target="tpu_custom_call" | custom-call | tf_op jit(solution)/shard_map/pallas_call | solution.py:564
  66.1 1.3 %shard_map.105 = (f32[1,512]{1,0:T(1,128)}, f32[3,512]{1,0:T(4,128)}) custom-call(f32[4,512]{1,0:T(4,128)} %shard_map.104.total_ref, f32[1,512]{1,0:T(1,128)} %bitcast.5, s32[1]{0:T(128)S(6)} %copy.11.counts_ref), custom_call_target="tpu_custom_call" | custom-call | tf_op jit(solution)/shard_map/pallas_call | solution.py:599

commit v7 on v6

--- a/solution.py
+++ b/solution.py
@@ -370,8 +370,9 @@
     for half in range(HALVES):
         turned_ref[half, :, place] = send_ref[half, :, :, place]
 
-    for member in far + near + [(side, 0, col)]:
-        prepare_slopes(block(member), member[1])
+    for member in far + near:
+        if member[0] is away:
+            prepare_slopes(block(member), member[1])
     fetches[2].wait()
     fetches[3].wait()
     back_flat = back_ref.reshape(HALVES, KX * PART, CZ)
@@ -398,24 +399,27 @@
         high, low = split(field)
         spectrum = influence * dot3(table_x_ref[0, :KX], table_x_ref[1, :KX], high, low)
         high, low = split(spectrum)
-        result = dot3(table_x_ref[0, :KX], table_x_ref[1, :KX], high, low)
-        for j in range(PART):
-            back_flat[half, pl.ds(j, KX, stride=PART), :] = result[:, j * CZ : (j + 1) * CZ]
-
         if half < HALVES - 1:
-            pieces = [slice(0, SIDES)]
+            pieces = [(slice(0, SIDES), 0, KX)]
         else:
-            pieces = [away, side]
-        for number, here in enumerate(pieces):
+            pieces = [(here, here * (KX // SIDES), KX // SIDES) for here in (away, side)]
+        for number, (here, start, rows) in enumerate(pieces):
+            if half < HALVES - 1:
+                lines = pl.ds(0, KX)
+            else:
+                lines = pl.ds(pl.multiple_of(start, KX // SIDES), rows)
+            result = dot3(table_x_ref[0, lines], table_x_ref[1, lines], high, low)
+            for j in range(PART):
+                back_flat[half, pl.ds(start * PART + j, rows, stride=PART), :] = result[
+                    :, j * CZ : (j + 1) * CZ
+                ]
 
             @pl.loop(1, SIDE)
             def _(step):
                 target = lax.rem(place + step, SIDE)
-                source = back_ref.at[half, here, target]
-                landing = returned_ref.at[half, here, :, place]
                 remote(
-                    source,
-                    landing,
+                    back_ref.at[half, here, target],
+                    returned_ref.at[half, here, :, place],
                     send_sems.at[2],
                     returned_sems.at[half + number],
                     side * SIDE + target,
@@ -424,7 +428,11 @@
 
         returned_ref[half, :, :, place] = back_ref[half, :, place]
 
+    for member in far + near + [(side, 0, col)]:
+        if member[0] is side:
+            prepare_slopes(block(member), member[1])
     fetches[4].wait()
+
     def returned(half, here, number):
         remote(
             returned_ref.at[half, here, :, 0 : SIDE - 1],

time: 67.6 us -> 67.6 us (level)
  no operation moved by 1% of the time
where the time goes in v7:
time: 67.6 us; the launch traced here: 67.4 us
  Pallas kernels  66.1 us (98%)
  between operations  1.29 us (2%)
    pallas_call x1, Pallas kernels, per_device(): pl.pallas_call(kernel, out_shape=shape((4, SLOTS)), in_specs=[vector, vec...  64.8 us

profile of v7, /device:TPU:1, one launch (start us, length us, event | category | flops | bytes accessed | tf_op | source)
XLA Modules:
  0.0 67.4 jit_solution(13220306919648549027)
XLA Ops:
  1.3 64.8 %shard_map.104.total_ref = f32[4,512]{1,0:T(4,128)} custom-call(f32[1,512]{1,0:T(1,128)} %bitcast.4, f32[3,512]{1,0:T(4,128)} %fractions_ref.1, s32[3,512]{1,0:T(4,128)} %cells_ref.1, s32[1]{0:T(128)S(6)} %copy.11.counts_ref, f32[1536,128]{1,0:T(8,128)} %bitcast.3, bf16[2,392,384]{2,1,0:T(8,128)(2,1)} %constant.8.clone.table_x_hbm, ...), custom_call_target="tpu_custom_call" | custom-call | tf_op jit(solution)/shard_map/pallas_call | solution.py:572
  66.1 1.3 %shard_map.105 = (f32[1,512]{1,0:T(1,128)}, f32[3,512]{1,0:T(4,128)}) custom-call(f32[4,512]{1,0:T(4,128)} %shard_map.104.total_ref, f32[1,512]{1,0:T(1,128)} %bitcast.5, s32[1]{0:T(128)S(6)} %copy.11.counts_ref), custom_call_target="tpu_custom_call" | custom-call | tf_op jit(solution)/shard_map/pallas_call | solution.py:607

commit v8 on v6

--- a/solution.py
+++ b/solution.py
@@ -24,7 +24,7 @@
 COARSE = KZ // FINE
 FAN = 2 * FINE
 VMEM_LIMIT = 63 * 1024 * 1024
-HALVES = 2
+HALVES = 1
 WIDTH = KY // ROWS
 PART = WIDTH // HALVES
 SIDES = 2

time: 67.6 us -> 67.9 us (level)
  no operation moved by 1% of the time
where the time goes in v8:
time: 67.9 us; the launch traced here: 67.6 us
  Pallas kernels  66.3 us (98%)
  between operations  1.29 us (2%)
    pallas_call x1, Pallas kernels, per_device(): pl.pallas_call(kernel, out_shape=shape((4, SLOTS)), in_specs=[vector, vec...  65 us

profile of v8, /device:TPU:1, one launch (start us, length us, event | category | flops | bytes accessed | tf_op | source)
XLA Modules:
  0.0 67.6 jit_solution(3703018075302075221)
XLA Ops:
  1.3 65.0 %shard_map.104.total_ref = f32[4,512]{1,0:T(4,128)} custom-call(f32[1,512]{1,0:T(1,128)} %bitcast.4, f32[3,512]{1,0:T(4,128)} %fractions_ref.1, s32[3,512]{1,0:T(4,128)} %cells_ref.1, s32[1]{0:T(128)S(6)} %copy.11.counts_ref, f32[1536,128]{1,0:T(8,128)} %bitcast.3, bf16[2,392,384]{2,1,0:T(8,128)(2,1)} %constant.8.clone.table_x_hbm, ...), custom_call_target="tpu_custom_call" | custom-call | tf_op jit(solution)/shard_map/pallas_call | solution.py:564
  66.3 1.3 %shard_map.105 = (f32[1,512]{1,0:T(1,128)}, f32[3,512]{1,0:T(4,128)}) custom-call(f32[4,512]{1,0:T(4,128)} %shard_map.104.total_ref, f32[1,512]{1,0:T(1,128)} %bitcast.5, s32[1]{0:T(128)S(6)} %copy.11.counts_ref), custom_call_target="tpu_custom_call" | custom-call | tf_op jit(solution)/shard_map/pallas_call | solution.py:599
